TPU v7x, 512 devices: a whole 4x4x16 slice. The times are simulated.
512 devices in a mesh: tan: 16 (over z), rad: 16 (over x_lo, y, core), inst: 2 (over x_hi).
Axes of the slice: x: 4 (x_hi: 2, x_lo: 2; x = x_hi * 2 + x_lo), y: 4, z: 16, core: 2. Of those that a mesh axis runs over, the one named last changes fastest.
Arguments:
- coords: float32 [2, 3, 512, 8, 2048], P('inst', None, 'rad', None, 'tan'), may hold values from -533 to 533, as said below
- state: float32 [2, 5, 512, 8, 2048], P('inst', None, 'rad', None, 'tan'), may hold values from -6 to 6
- spectral_rest: float32 [2, 5, 512, 8, 2048], P('inst', None, 'rad', None, 'tan'), may hold values from -4 to 4
- instance_ids: int32 [2], replicated, may hold values from 0 to 15, as said below
- motion: float32 [2], replicated, may hold values from 0.2 to 0.6
- heave: float32 [3], replicated, may hold values from -3 to 3
- free_stream: float32 [3], replicated, may hold values from -3 to 3
Outputs:
- displacement: float32 [2, 3, 512, 8, 2048], P('inst', None, 'rad', None, 'tan')
- residual: float32 [2, 5, 512, 8, 2048], P('inst', None, 'rad', None, 'tan')
Inputs may be any that keep to these rules, and one draw needn't show every extreme that they name: `instance_ids`: one of the two instance numbers is 15; the other lies 1 to 3 instances away from it, modulo 16. `coords`: points of an O-grid around a body, radial distance rising along j.
All inputs are finite; a program needn't handle non-finite values.
Results may differ from a plain program's by a relative error of at most 0.0003.
Values sent between devices are 32-bit elements; how exact they have to be, the bound alone decides.
A program may use at most 64 MiB of HBM per device.

v0:
```python
import jax
import jax.numpy as jnp
from jax import lax
from jax.sharding import PartitionSpec as P

NINST = 16


coef_two = 0.1
coef_four = 0.05


def from_behind(block, axis, distance):
    devices = range(lax.axis_size(axis))
    route = [(i - distance, i) for i in devices if i - distance in devices]
    return lax.ppermute(block, axis, route)


def carried_in(value, axis, combine, identity):
    peers, index = (lax.axis_size(axis), lax.axis_index(axis))
    everything = lax.all_gather(value, axis)
    start = jnp.broadcast_to(jnp.asarray(identity, value.dtype), value.shape)

    def hop(k, before):
        reached = k < index
        new = combine(before, everything[k])
        return jnp.where(reached, new, before)

    return lax.fori_loop(0, peers, hop, start)


def spread(value, axis, root):
    mine = lax.axis_index(axis) == root
    return lax.psum(jnp.where(mine, value, jnp.zeros_like(value)), axis)


def with_halo(value, sides, width):
    for axis, dim in sides:
        peers, length = (lax.axis_size(axis), value.shape[dim])
        up = [(i, (i + 1) % peers) for i in range(peers)]
        down = [(j, i) for i, j in up]
        last = lax.slice_in_dim(value, length - width, length, axis=dim)
        leading = lax.slice_in_dim(value, 0, width, axis=dim)
        before = lax.ppermute(last, axis, up)
        after = lax.ppermute(leading, axis, down)
        value = jnp.concatenate([before, value, after], axis=dim)
    return value


def swapped(value, axis, stride):
    mask = 2**stride
    pairs = [(source, source ^ mask) for source in range(lax.axis_size(axis))]
    return lax.ppermute(value, axis, pairs)


def axis_slope(field, axis):
    count = field.shape[axis]
    first = lax.slice_in_dim(field, 1, 2, axis=axis) - lax.slice_in_dim(field, 0, 1, axis=axis)
    middle = (
        lax.slice_in_dim(field, 2, count, axis=axis)
        - lax.slice_in_dim(field, 0, count - 2, axis=axis)
    ) * 0.5
    last = lax.slice_in_dim(field, count - 1, count, axis=axis) - lax.slice_in_dim(
        field, count - 2, count - 1, axis=axis
    )
    return jnp.concatenate([first, middle, last], axis=axis)


def triple(rad_vec, tan_vec, span_vec):
    return (
        rad_vec[0] * (tan_vec[1] * span_vec[2] - tan_vec[2] * span_vec[1])
        + rad_vec[1] * (tan_vec[2] * span_vec[0] - tan_vec[0] * span_vec[2])
        + rad_vec[2] * (tan_vec[0] * span_vec[1] - tan_vec[1] * span_vec[0])
    )


def jst_term(minus_two, minus_one, centre, plus_one, plus_two, speed):
    press_minus = 1.0 + minus_one[0] * minus_one[0]
    press_centre = 1.0 + centre[0] * centre[0]
    press_plus = 1.0 + plus_one[0] * plus_one[0]
    sensor = (
        coef_two
        * jnp.abs(press_plus - 2.0 * press_centre + press_minus)
        / (press_plus + 2.0 * press_centre + press_minus)
    )
    fourth = jnp.maximum(0.0, coef_four - sensor)
    second_diff = plus_one - 2.0 * centre + minus_one
    fourth_diff = plus_two - 4.0 * plus_one + 6.0 * centre - 4.0 * minus_one + minus_two
    return speed * 0.5 * (plus_one - minus_one) - jnp.abs(speed) * (
        sensor * second_diff - fourth * fourth_diff
    )


def spectral_coef(offset):
    angle = jnp.pi * offset.astype(jnp.float32) / NINST
    parity = 1.0 - 2.0 * (offset % 2).astype(jnp.float32)
    return 0.5 * parity * jnp.cos(angle) / jnp.sin(angle)


def body(coords, state, spectral_rest, instance_ids, motion, heave, free_stream):
    grid = coords[0]
    flow = state[0]
    rest_term = spectral_rest[0]
    rad_count = lax.axis_size("rad")
    rad_place = lax.axis_index("rad")
    inst_place = lax.axis_index("inst")
    depth = grid.shape[1]
    width = grid.shape[3]
    prior = from_behind(grid[:, depth - 1 :], "rad", 1)
    below = jnp.concatenate([prior, grid[:, : depth - 1]], axis=1)
    seg = jnp.sqrt(jnp.sum((grid - below) ** 2, axis=0))
    layer = jnp.arange(depth)[:, None, None]
    seg = jnp.where((layer == 0) & (rad_place == 0), 0.0, seg)
    cumul = jnp.cumsum(seg, axis=0)
    line_sum = cumul[depth - 1]
    offset = carried_in(
        line_sum, "rad", lambda earlier, later: earlier + later, jnp.zeros_like(line_sum)
    )
    total = lax.psum(line_sum, "rad")
    frac = (offset[None] + cumul) / total[None]
    own_id = instance_ids[inst_place]
    other_id = instance_ids[1 - inst_place]
    phase = 2.0 * jnp.pi * own_id.astype(jnp.float32) / NINST + motion[1]
    theta = motion[0] * jnp.sin(phase)
    wall = grid[:, 0]
    wall_y = wall[1] * jnp.cos(theta) - wall[2] * jnp.sin(theta) - wall[1]
    wall_z = wall[1] * jnp.sin(theta) + wall[2] * jnp.cos(theta) - wall[2]
    wall_disp = jnp.stack([jnp.zeros_like(wall_y), wall_y, wall_z])
    wall_disp = spread(wall_disp, "rad", 0)
    far = heave * jnp.cos(phase)
    disp = (1.0 - frac)[None] * wall_disp[:, None] + frac[None] * far[:, None, None, None]
    moved = grid + disp
    flow_ext = with_halo(flow, (("rad", 1), ("tan", 3)), 2)
    coord_ext = with_halo(moved, (("rad", 1), ("tan", 3)), 1)
    rows = jnp.arange(depth + 4)
    keep = jnp.logical_not(
        (rows < 2) & (rad_place == 0) | (rows >= depth + 2) & (rad_place == rad_count - 1)
    )
    flow_ext = jnp.where(keep[None, :, None, None], flow_ext, 0.0)
    tan_vec = (coord_ext[:, 1 : depth + 1, :, 2:] - coord_ext[:, 1 : depth + 1, :, :width]) * 0.5
    upper = coord_ext[:, 2:, :, 1 : width + 1]
    lower_pts = coord_ext[:, :depth, :, 1 : width + 1]
    centre_pts = coord_ext[:, 1 : depth + 1, :, 1 : width + 1]
    local_row = jnp.arange(depth)[None, :, None, None]
    at_wall = (local_row == 0) & (rad_place == 0)
    at_far = (local_row == depth - 1) & (rad_place == rad_count - 1)
    rad_vec = jnp.where(
        at_wall,
        upper - centre_pts,
        jnp.where(at_far, centre_pts - lower_pts, (upper - lower_pts) * 0.5),
    )
    span_vec = axis_slope(moved, 2)
    volume = triple(rad_vec, tan_vec, span_vec)
    pair = swapped(jnp.concatenate([disp, volume[None] * flow], axis=0), "inst", 0)
    other_disp = pair[:3]
    other_weighted = pair[3:]
    coef = spectral_coef(own_id - other_id)
    relative = free_stream[:, None, None, None] - coef * other_disp
    speed_tan = jnp.sum(relative * tan_vec, axis=0)
    speed_rad = jnp.sum(relative * rad_vec, axis=0)
    along_tan = flow_ext[:, 2 : depth + 2]
    along_rad = flow_ext[:, :, :, 2 : width + 2]
    term_tan = jst_term(
        along_tan[..., 0:width],
        along_tan[..., 1 : width + 1],
        along_tan[..., 2 : width + 2],
        along_tan[..., 3 : width + 3],
        along_tan[..., 4 : width + 4],
        speed_tan,
    )
    term_rad = jst_term(
        along_rad[:, 0:depth],
        along_rad[:, 1 : depth + 1],
        along_rad[:, 2 : depth + 2],
        along_rad[:, 3 : depth + 3],
        along_rad[:, 4 : depth + 4],
        speed_rad,
    )
    result = term_tan + term_rad + coef * other_weighted + rest_term
    return (disp[None], result[None])


def solution(mesh):
    return jax.shard_map(
        body,
        mesh=mesh,
        in_specs=(
            P("inst", None, "rad", None, "tan"),
            P("inst", None, "rad", None, "tan"),
            P("inst", None, "rad", None, "tan"),
            P(),
            P(),
            P(),
            P(),
        ),
        out_specs=(P("inst", None, "rad", None, "tan"), P("inst", None, "rad", None, "tan")),
        check_vma=False,
    )
```

profile of v0, /device:TPU:6, one launch (start us, length us, event | category | flops | bytes accessed | tf_op | source)
XLA Modules:
  0.0 155.4 jit_solution(15402254528347595846)
XLA Ops:
  0.6 0.7 slice.245
  1.4 1.9 %collective-permute-start = (f32[3,1,8,128]{3,2,1,0:T(8,128)S(1)}, f32[3,1,8,128]{3,2,1,0:T(8,128)S(1)}, u32[]{:S(2)}, u32[]{:S(2)}) collective-permute-start(f32[3,1,8,128]{3,2,1,0:T(8,128)S(1)} %slice.245), channel_id=1, source_target_pairs={{0,2},{2,4},{4,6},{6,8},{8,10},{10,12},{12,14},{14,16},{16,18},{18... | collective-permute-start | bytes 36872 | tf_op jit(solution)/shard_map/ppermute | solution.py:16
  3.3 0.9 fusion.44
  4.1 3.6 %collective-permute-start.6 = (f32[5,2,8,128]{3,2,1,0:T(8,128)S(1)}, f32[5,2,8,128]{3,2,1,0:T(8,128)S(1)}, u32[]{:S(2)}, u32[]{:S(2)}) collective-permute-start(f32[5,2,8,128]{3,2,1,0:T(8,128)S(1)} %get-tuple-element.121), channel_id=1, source_target_pairs={{0,2},{2,4},{4,6},{6,8},{8,10},{10,12},{12,14},{14,16},{16,18},{18... | collective-permute-start | bytes 122888 | tf_op jit(solution)/shard_map/ppermute | solution.py:44
  7.7 4.1 %collective-permute-start.7 = (f32[5,2,8,128]{3,2,1,0:T(8,128)S(1)}, f32[5,2,8,128]{3,2,1,0:T(8,128)S(1)}, u32[]{:S(2)}, u32[]{:S(2)}) collective-permute-start(f32[5,2,8,128]{3,2,1,0:T(8,128)S(1)} %get-tuple-element.122), channel_id=1, source_target_pairs={{2,0},{4,2},{6,4},{8,6},{10,8},{12,10},{14,12},{16,14},{18,16},{20... | collective-permute-start | bytes 122888 | tf_op jit(solution)/shard_map/ppermute | solution.py:45
  11.8 1.3 fusion.48
  13.8 1.3 fusion.49
  16.6 0.7 subtract_subtract_fusion
  17.3 0.7 broadcast_multiply_fusion.3
  18.0 0.1 maximum_select_fusion.1
  18.1 1.0 slice.246
  20.6 1.1 fusion.27
  21.7 0.1 fusion.37
  21.8 17.3 %all_gather.3 = f32[16,8,128]{2,1,0:T(8,128)S(1)} all-gather(f32[1,8,128]{2,1,0:T(8,128)S(1)} %get-tuple-element.139), channel_id=1, replica_groups=mesh['tan'=16,'rad'=16,'inst'=2] {'rad'}, dimensions={0}, use_global_device_ids=true | all-gather | bytes 69632 | tf_op jit(solution)/shard_map/all_gather | solution.py:21
  39.1 0.5 while.14
  39.6 53.6 %all-reduce = (f32[8,128]{1,0:T(8,128)S(1)}, f32[3,8,128]{2,1,0:T(8,128)S(1)}) all-reduce(f32[8,128]{1,0:T(8,128)S(1)} %get-tuple-element.140, f32[3,8,128]{2,1,0:T(8,128)S(1)} %maximum_select_fusion.1), channel_id=1, replica_groups=mesh['tan'=16,'rad'=16,'inst'=2] {'rad'}, use_global_device_ids=true, to_apply=%region_4.5 | all-reduce | flops 4096 | bytes 32768 | tf_op jit(solution)/shard_map/psum | solution.py:119
  93.3 0.1 multiply_add_fusion
  93.4 0.1 fusion.17
  93.5 1.9 %collective-permute-start.1 = (f32[3,1,8,128]{3,2,1,0:T(8,128)S(1)}, f32[3,1,8,128]{3,2,1,0:T(8,128)S(1)}, u32[]{:S(2)}, u32[]{:S(2)}) collective-permute-start(f32[3,1,8,128]{3,2,1,0:T(8,128)S(1)} %get-tuple-element.129), channel_id=1, source_target_pairs={{2,0},{4,2},{6,4},{8,6},{10,8},{12,10},{14,12},{16,14},{18,16},{20... | collective-permute-start | bytes 36872 | tf_op jit(solution)/shard_map/ppermute | solution.py:45
  95.4 2.4 %collective-permute-start.2 = (f32[3,1,8,128]{3,2,1,0:T(8,128)S(1)}, f32[3,1,8,128]{3,2,1,0:T(8,128)S(1)}, u32[]{:S(2)}, u32[]{:S(2)}) collective-permute-start(f32[3,1,8,128]{3,2,1,0:T(8,128)S(1)} %get-tuple-element.130), channel_id=1, source_target_pairs={{0,2},{2,4},{4,6},{6,8},{8,10},{10,12},{12,14},{14,16},{16,18},{18... | collective-permute-start | bytes 36872 | tf_op jit(solution)/shard_map/ppermute | solution.py:44
  97.8 0.1 slice_subtract_fusion.4
  98.0 4.6 %collective-permute-done.2 = f32[3,1,8,128]{3,2,1,0:T(8,128)S(1)} collective-permute-done((f32[3,1,8,128]{3,2,1,0:T(8,128)S(1)}, f32[3,1,8,128]{3,2,1,0:T(8,128)S(1)}, u32[]{:S(2)}, u32[]{:S(2)}) %collective-permute-start.2) | collective-permute-done | bytes 12320 | tf_op jit(solution)/shard_map/ppermute | solution.py:44
  102.6 0.2 fusion.45
  102.8 11.4 %collective-permute-start.3 = (f32[3,34,8,1]{3,2,1,0:T(8,128)S(1)}, f32[3,34,8,1]{3,2,1,0:T(8,128)S(1)}, u32[]{:S(2)}, u32[]{:S(2)}) collective-permute-start(f32[3,34,8,1]{3,2,1,0:T(8,128)S(1)} %get-tuple-element.125), channel_id=1, source_target_pairs={{32,0},{64,32},{96,64},{128,96},{160,128},{192,160},{224,192},{256... | collective-permute-start | bytes 9800 | tf_op jit(solution)/shard_map/ppermute | solution.py:45
  114.2 1.9 %collective-permute-start.4 = (f32[3,34,8,1]{3,2,1,0:T(8,128)S(1)}, f32[3,34,8,1]{3,2,1,0:T(8,128)S(1)}, u32[]{:S(2)}, u32[]{:S(2)}) collective-permute-start(f32[3,34,8,1]{3,2,1,0:T(8,128)S(1)} %get-tuple-element.126), channel_id=1, source_target_pairs={{0,32},{32,64},{64,96},{96,128},{128,160},{160,192},{192,224},{224... | collective-permute-start | bytes 9800 | tf_op jit(solution)/shard_map/ppermute | solution.py:44
  116.1 0.1 pad_maximum_fusion.11
  116.3 3.5 %collective-permute-done.3 = f32[3,34,8,1]{3,2,1,0:T(8,128)S(1)} collective-permute-done((f32[3,34,8,1]{3,2,1,0:T(8,128)S(1)}, f32[3,34,8,1]{3,2,1,0:T(8,128)S(1)}, u32[]{:S(2)}, u32[]{:S(2)}) %collective-permute-start.3) | collective-permute-done | bytes 3296 | tf_op jit(solution)/shard_map/ppermute | solution.py:45
  119.7 5.6 %collective-permute-done.4 = f32[3,34,8,1]{3,2,1,0:T(8,128)S(1)} collective-permute-done((f32[3,34,8,1]{3,2,1,0:T(8,128)S(1)}, f32[3,34,8,1]{3,2,1,0:T(8,128)S(1)}, u32[]{:S(2)}, u32[]{:S(2)}) %collective-permute-start.4) | collective-permute-done | bytes 3296 | tf_op jit(solution)/shard_map/ppermute | solution.py:44
  125.3 0.5 fusion.19
  125.8 0.1 fusion.35
  125.9 0.1 broadcast_multiply_fusion
  126.0 1.1 pad_maximum_fusion
  127.0 3.3 %collective-permute-start.5 = (f32[8,32,8,128]{3,2,1,0:T(8,128)}, f32[8,32,8,128]{3,2,1,0:T(8,128)}, u32[]{:S(2)}, u32[]{:S(2)}) collective-permute-start(f32[8,32,8,128]{3,2,1,0:T(8,128)} %pad_maximum_fusion), channel_id=1, source_target_pairs={{0,1},{1,0},{2,3},{3,2},{4,5},{5,4},{6,7},{7,6},{8,9},{9,8},{10,11... | collective-permute-start | bytes 3145736 | tf_op jit(solution)/shard_map/ppermute | solution.py:53
  130.3 0.1 pad_maximum_fusion.1
  130.4 0.3 fusion.43
  130.7 0.4 copy.17
  131.0 1.9 %collective-permute-start.8 = (f32[5,36,8,2]{1,2,3,0:T(8,128)S(1)}, f32[5,36,8,2]{1,2,3,0:T(8,128)S(1)}, u32[]{:S(2)}, u32[]{:S(2)}) collective-permute-start(f32[5,36,8,2]{1,2,3,0:T(8,128)S(1)} %copy.17), channel_id=1, source_target_pairs={{0,32},{32,64},{64,96},{96,128},{128,160},{160,192},{192,224},{224... | collective-permute-start | bytes 34568 | tf_op jit(solution)/shard_map/ppermute | solution.py:44
  133.0 0.4 copy.18
  133.4 5.1 %collective-permute-start.9 = (f32[5,36,8,2]{1,2,3,0:T(8,128)S(1)}, f32[5,36,8,2]{1,2,3,0:T(8,128)S(1)}, u32[]{:S(2)}, u32[]{:S(2)}) collective-permute-start(f32[5,36,8,2]{1,2,3,0:T(8,128)S(1)} %copy.18), channel_id=1, source_target_pairs={{32,0},{64,32},{96,64},{128,96},{160,128},{192,160},{224,192},{256... | collective-permute-start | bytes 34568 | tf_op jit(solution)/shard_map/ppermute | solution.py:45
  138.5 0.8 multiply_add_fusion.1
  139.3 0.4 copy.19
  139.8 0.4 collective-permute-done.9
  140.1 0.4 copy.20
  140.6 0.7 maximum_select_fusion
  141.3 0.3 maximum_bitcast_fusion.1
  141.5 9.3 %collective-permute-done.5 = f32[8,32,8,128]{3,2,1,0:T(8,128)} collective-permute-done((f32[8,32,8,128]{3,2,1,0:T(8,128)}, f32[8,32,8,128]{3,2,1,0:T(8,128)}, u32[]{:S(2)}, u32[]{:S(2)}) %collective-permute-start.5) | collective-permute-done | bytes 1048608 | tf_op jit(solution)/shard_map/ppermute | solution.py:53
  150.8 1.2 multiply_reduce_fusion.1
  152.0 3.4 %fusion.2 = f32[1,5,32,8,128]{4,3,2,1,0:T(8,128)} fusion(f32[8,32,8,128]{3,2,1,0:T(8,128)} %collective-permute-done.5, f32[5,36,8,132]{3,2,1,0:T(8,128)S(1)} %maximum_select_fusion, f32[1,5,32,8,128]{4,3,2,1,0:T(8,128)S(1)} %copy-done.2, f32[]{:T(128)S(6)} %div.38, f32[32,8,128]{2,1,0:T(8,128)S(1)} %get-tuple-element.117, f32[32,8,128]{2,1,0:T(8,128)S(1)} %bitcast.47, ...), kind=kLoop, calls=%fused_computation.7 | loop fusion | flops 5898240 | bytes 8912900 | tf_op jit(solution)/shard_map/broadcast_in_dim | solution.py:180
  (39 shorter events, 0.3 us)
Async XLA Ops:
  1.4 19.3 %collective-permute-start = (f32[3,1,8,128]{3,2,1,0:T(8,128)S(1)}, f32[3,1,8,128]{3,2,1,0:T(8,128)S(1)}, u32[]{:S(2)}, u32[]{:S(2)}) collective-permute-start(f32[3,1,8,128]{3,2,1,0:T(8,128)S(1)} %slice.245), channel_id=1, source_target_pairs={{0,2},{2,4},{4,6},{6,8},{8,10},{10,12},{12,14},{14,16},{16,18},{18... | collective-permute-start | bytes 36872 | tf_op jit(solution)/shard_map/ppermute | solution.py:16
  3.3 90.0 %copy-start.1 = (f32[1,3,32,8,128]{4,3,2,1,0:T(8,128)S(1)}, f32[1,3,32,8,128]{4,3,2,1,0:T(8,128)}, u32[]{:S(2)}) copy-start(f32[1,3,32,8,128]{4,3,2,1,0:T(8,128)} %param.9) | copy-start | bytes 1179652
  4.1 126.2 %collective-permute-start.6 = (f32[5,2,8,128]{3,2,1,0:T(8,128)S(1)}, f32[5,2,8,128]{3,2,1,0:T(8,128)S(1)}, u32[]{:S(2)}, u32[]{:S(2)}) collective-permute-start(f32[5,2,8,128]{3,2,1,0:T(8,128)S(1)} %get-tuple-element.121), channel_id=1, source_target_pairs={{0,2},{2,4},{4,6},{6,8},{8,10},{10,12},{12,14},{14,16},{16,18},{18... | collective-permute-start | bytes 122888 | tf_op jit(solution)/shard_map/ppermute | solution.py:44
  7.7 122.6 %collective-permute-start.7 = (f32[5,2,8,128]{3,2,1,0:T(8,128)S(1)}, f32[5,2,8,128]{3,2,1,0:T(8,128)S(1)}, u32[]{:S(2)}, u32[]{:S(2)}) collective-permute-start(f32[5,2,8,128]{3,2,1,0:T(8,128)S(1)} %get-tuple-element.122), channel_id=1, source_target_pairs={{2,0},{4,2},{6,4},{8,6},{10,8},{12,10},{14,12},{16,14},{18,16},{20... | collective-permute-start | bytes 122888 | tf_op jit(solution)/shard_map/ppermute | solution.py:45
  93.5 4.5 %collective-permute-start.1 = (f32[3,1,8,128]{3,2,1,0:T(8,128)S(1)}, f32[3,1,8,128]{3,2,1,0:T(8,128)S(1)}, u32[]{:S(2)}, u32[]{:S(2)}) collective-permute-start(f32[3,1,8,128]{3,2,1,0:T(8,128)S(1)} %get-tuple-element.129), channel_id=1, source_target_pairs={{2,0},{4,2},{6,4},{8,6},{10,8},{12,10},{14,12},{16,14},{18,16},{20... | collective-permute-start | bytes 36872 | tf_op jit(solution)/shard_map/ppermute | solution.py:45
  95.4 7.1 %collective-permute-start.2 = (f32[3,1,8,128]{3,2,1,0:T(8,128)S(1)}, f32[3,1,8,128]{3,2,1,0:T(8,128)S(1)}, u32[]{:S(2)}, u32[]{:S(2)}) collective-permute-start(f32[3,1,8,128]{3,2,1,0:T(8,128)S(1)} %get-tuple-element.130), channel_id=1, source_target_pairs={{0,2},{2,4},{4,6},{6,8},{8,10},{10,12},{12,14},{14,16},{16,18},{18... | collective-permute-start | bytes 36872 | tf_op jit(solution)/shard_map/ppermute | solution.py:44
  102.8 16.9 %collective-permute-start.3 = (f32[3,34,8,1]{3,2,1,0:T(8,128)S(1)}, f32[3,34,8,1]{3,2,1,0:T(8,128)S(1)}, u32[]{:S(2)}, u32[]{:S(2)}) collective-permute-start(f32[3,34,8,1]{3,2,1,0:T(8,128)S(1)} %get-tuple-element.125), channel_id=1, source_target_pairs={{32,0},{64,32},{96,64},{128,96},{160,128},{192,160},{224,192},{256... | collective-permute-start | bytes 9800 | tf_op jit(solution)/shard_map/ppermute | solution.py:45
  114.2 11.1 %collective-permute-start.4 = (f32[3,34,8,1]{3,2,1,0:T(8,128)S(1)}, f32[3,34,8,1]{3,2,1,0:T(8,128)S(1)}, u32[]{:S(2)}, u32[]{:S(2)}) collective-permute-start(f32[3,34,8,1]{3,2,1,0:T(8,128)S(1)} %get-tuple-element.126), channel_id=1, source_target_pairs={{0,32},{32,64},{64,96},{96,128},{128,160},{160,192},{192,224},{224... | collective-permute-start | bytes 9800 | tf_op jit(solution)/shard_map/ppermute | solution.py:44
  116.2 9.6 %copy-start = (f32[1,5,32,8,128]{4,3,2,1,0:T(8,128)S(1)}, f32[1,5,32,8,128]{4,3,2,1,0:T(8,128)}, u32[]{:S(2)}) copy-start(f32[1,5,32,8,128]{4,3,2,1,0:T(8,128)} %param.10) | copy-start | bytes 1966084
  127.0 23.8 %collective-permute-start.5 = (f32[8,32,8,128]{3,2,1,0:T(8,128)}, f32[8,32,8,128]{3,2,1,0:T(8,128)}, u32[]{:S(2)}, u32[]{:S(2)}) collective-permute-start(f32[8,32,8,128]{3,2,1,0:T(8,128)} %pad_maximum_fusion), channel_id=1, source_target_pairs={{0,1},{1,0},{2,3},{3,2},{4,5},{5,4},{6,7},{7,6},{8,9},{9,8},{10,11... | collective-permute-start | bytes 3145736 | tf_op jit(solution)/shard_map/ppermute | solution.py:53
  131.0 8.3 %collective-permute-start.8 = (f32[5,36,8,2]{1,2,3,0:T(8,128)S(1)}, f32[5,36,8,2]{1,2,3,0:T(8,128)S(1)}, u32[]{:S(2)}, u32[]{:S(2)}) collective-permute-start(f32[5,36,8,2]{1,2,3,0:T(8,128)S(1)} %copy.17), channel_id=1, source_target_pairs={{0,32},{32,64},{64,96},{96,128},{128,160},{160,192},{192,224},{224... | collective-permute-start | bytes 34568 | tf_op jit(solution)/shard_map/ppermute | solution.py:44
  133.4 6.8 %collective-permute-start.9 = (f32[5,36,8,2]{1,2,3,0:T(8,128)S(1)}, f32[5,36,8,2]{1,2,3,0:T(8,128)S(1)}, u32[]{:S(2)}, u32[]{:S(2)}) collective-permute-start(f32[5,36,8,2]{1,2,3,0:T(8,128)S(1)} %copy.18), channel_id=1, source_target_pairs={{32,0},{64,32},{96,64},{128,96},{160,128},{192,160},{224,192},{256... | collective-permute-start | bytes 34568 | tf_op jit(solution)/shard_map/ppermute | solution.py:45
  140.6 10.2 %copy-start.3 = (f32[3]{0:T(128)S(1)}, f32[3]{0:T(128)}, u32[]{:S(2)}) copy-start(f32[3]{0:T(128)} %param.15) | copy-start | bytes 40
  141.3 10.8 %copy-start.2 = (f32[1,5,32,8,128]{4,3,2,1,0:T(8,128)S(1)}, f32[1,5,32,8,128]{4,3,2,1,0:T(8,128)}, u32[]{:S(2)}) copy-start(f32[1,5,32,8,128]{4,3,2,1,0:T(8,128)} %param.11) | copy-start | bytes 1966084
where the time goes:
time: 156 us; the launch traced here: 155 us
  blocking collectives  70.9 us (45%)
  starting transfers between devices  37.6 us (24%)
  waiting for transfers between devices  23.3 us (15%)
  other arithmetic  11.3 us (7%)
  local copies, waits for them, and re-layouts  7.28 us (5%)
  between operations  4.63 us (3%)
    psum x1, blocking collectives, body(): total = lax.psum(line_sum, 'rad')  53.6 us
    ppermute x4, starting transfers between devices, with_halo(): after = lax.ppermute(leading, axis, down)  22.5 us
    all_gather x1, blocking collectives, carried_in(): everything = lax.all_gather(value, axis)  17.3 us
    ppermute x4, waiting for transfers between devices, with_halo(): before = lax.ppermute(last, axis, up)  10.2 us
    ppermute x4, starting transfers between devices, with_halo(): before = lax.ppermute(last, axis, up)  9.82 us
    ppermute x1, waiting for transfers between devices, swapped(): return lax.ppermute(value, axis, pairs)  9.27 us
    ppermute x4, waiting for transfers between devices, with_halo(): after = lax.ppermute(leading, axis, down)  3.85 us
    broadcast_in_dim x1, other arithmetic, body(): return (disp[None], result[None])  3.35 us
  transfers between devices with their start and end apart: 10, of which 5 were waited for; matrix products, arithmetic and copies ran while one was open for 9% of the time, Pallas kernels for 0%

commit v1 on v0

v1 whole, which is shorter than its diff:
```python
import functools

import jax
import jax.numpy as jnp
from jax import lax
from jax.experimental import pallas as pl
from jax.experimental.pallas import tpu as pltpu
from jax.sharding import PartitionSpec as P

NINST = 16
COEF_TWO = 0.1
COEF_FOUR = 0.05
MESH = pl.DeviceIdType.MESH
ROWS = 32
CHUNKS = 4
TILE = (8, 128)


def send(src, dst, sems, slot, device):
    return pltpu.make_async_remote_copy(
        src_ref=src,
        dst_ref=dst,
        send_sem=sems[0].at[slot],
        recv_sem=sems[1].at[slot],
        device_id=device,
        device_id_type=MESH,
    )


def length(a, b):
    d = [p - q for p, q in zip(a, b)]
    return jnp.sqrt(d[0] * d[0] + d[1] * d[1] + d[2] * d[2])


def jst(m2, m1, c, p1, p2, speed):
    q_m, q_c, q_p = (1.0 + w[0] * w[0] for w in (m1, c, p1))
    outer = q_p + q_m
    sensor = COEF_TWO * jnp.abs(outer - 2.0 * q_c) / (outer + 2.0 * q_c)
    fourth = jnp.maximum(0.0, COEF_FOUR - sensor)
    size = jnp.abs(speed)
    half = 0.5 * speed
    near = size * (sensor + 4.0 * fourth)
    mid = size * (2.0 * sensor + 6.0 * fourth)
    far = size * fourth
    return [
        half * (p1[k] - m1[k]) - near * (p1[k] + m1[k]) + mid * c[k] + far * (p2[k] + m2[k])
        for k in range(5)
    ]


def step_kernel(
    nrad, ntan,
    coords, state, rest, ids, motion, heave, stream,
    disp_out, res_out,
    grid, flow, rest_v, moved, arc, frac_out, frac_in, e_t, e_r, vol_out, vol_in, state_in,
    wall, sums, cross_out, cross_in, flow_edge, flow_left, flow_right, move_edge, move_left, move_right,
    ids_s, motion_s, heave_s, stream_s,
    local, bulk_s, bulk_r, row_s, row_r, wall_s, wall_r, sum_s, sum_r, one_s, one_r,
):
    rad, tan, inst = lax.axis_index("rad"), lax.axis_index("tan"), lax.axis_index("inst")
    half = nrad // 2
    place, side = lax.rem(rad, half), rad // half
    first, last = rad == 0, rad == nrad - 1
    partner = {"inst": 1 - inst}
    left = {"tan": lax.rem(tan + ntan - 1, ntan)}
    right = {"tan": lax.rem(tan + 1, ntan)}
    above = {"rad": lax.rem(rad + 1, nrad)}
    below = {"rad": lax.rem(rad + nrad - 1, nrad)}
    across = {"rad": lax.rem(rad + half, nrad)}
    peers = [{"rad": side * half + lax.rem(place + k, half)} for k in range(1, half)]

    loads = [
        pltpu.make_async_copy(coords.at[0], grid.at[:, pl.ds(1, ROWS)], local.at[0]),
        pltpu.make_async_copy(state.at[0], flow.at[:, pl.ds(2, ROWS)], local.at[1]),
        pltpu.make_async_copy(rest.at[0], rest_v, local.at[2]),
        pltpu.make_async_copy(ids, ids_s, local.at[3]),
        pltpu.make_async_copy(motion, motion_s, local.at[4]),
        pltpu.make_async_copy(heave, heave_s, local.at[5]),
        pltpu.make_async_copy(stream, stream_s, local.at[6]),
    ]
    barrier = pltpu.get_barrier_semaphore()
    for device in [partner, left, right, across] + peers:
        pl.semaphore_signal(barrier, inc=1, device_id=device, device_id_type=MESH)

    @pl.when(rad == half - 1)
    def _():
        pl.semaphore_signal(barrier, inc=1, device_id=above, device_id_type=MESH)

    @pl.when(rad == half)
    def _():
        pl.semaphore_signal(barrier, inc=1, device_id=below, device_id_type=MESH)

    for load in loads:
        load.start()
    beyond = jnp.where((rad == half - 1) | (rad == half), 1, 0)
    pl.semaphore_wait(barrier, 4 + half - 1 + beyond)

    row = (row_s, row_r)
    to_above = [
        send(coords.at[0, :, ROWS - 1], grid.at[:, 0], row, 0, above),
        send(state.at[0, :, pl.ds(ROWS - 2, 2)], flow.at[:, pl.ds(0, 2)], row, 1, above),
    ]
    to_below = [
        send(coords.at[0, :, 0], grid.at[:, ROWS + 1], row, 2, below),
        send(state.at[0, :, pl.ds(0, 2)], flow.at[:, pl.ds(ROWS + 2, 2)], row, 3, below),
    ]
    walls = [
        send(coords.at[0, pl.ds(1, 2), 0], wall, (wall_s, wall_r), k, device)
        for k, device in enumerate([across] + peers)
    ]
    passed = [send(wall, wall, (wall_s, wall_r), k + 1, device) for k, device in enumerate(peers)]
    count = ROWS // CHUNKS
    bulk = [
        send(
            state.at[0, :, pl.ds(k * count, count)],
            state_in.at[:, pl.ds(k * count, count)],
            (bulk_s, bulk_r), k, partner,
        )
        for k in range(CHUNKS)
    ]

    @pl.when(rad < nrad - 1)
    def _():
        to_above[0].start()

    @pl.when(rad > 0)
    def _():
        to_below[0].start()

    @pl.when(first)
    def _():
        for copy in walls:
            copy.start()

    @pl.when(rad < nrad - 1)
    def _():
        to_above[1].start()

    @pl.when(rad > 0)
    def _():
        to_below[1].start()

    for copy in bulk:
        copy.start()

    lane = lax.broadcasted_iota(jnp.int32, TILE, 1)
    span = lax.broadcasted_iota(jnp.int32, TILE, 0)
    zero = jnp.zeros(TILE, jnp.float32)

    loads[0].wait()

    def inner(j, carry):
        before, total = carry[:3], carry[3]
        here = tuple(grid[c, j + 1] for c in range(3))
        total = total + length(here, before)
        arc[j] = total
        return (*here, total)

    arc[0] = zero
    top = lax.fori_loop(
        1, ROWS, inner, (*(grid[c, 1] for c in range(3)), zero), unroll=4
    )

    loads[1].wait()

    def pack_flow(j, edge):
        mine = lane // 4 == j
        return tuple(
            jnp.where(mine, pltpu.roll(flow[c, j + 2], 4 * j + 2, 1), edge[c]) for c in range(5)
        )

    edges = lax.fori_loop(0, ROWS, pack_flow, (zero,) * 5, unroll=4)
    for c in range(5):
        flow_edge[c] = edges[c]
    one = (one_s, one_r)
    flow_sends = [
        send(flow_edge, flow_left, one, 0, right),
        send(flow_edge, flow_right, one, 1, left),
    ]
    for copy in flow_sends:
        copy.start()

    for load in loads[3:]:
        load.wait()
    own_id = jnp.where(inst == 0, ids_s[0], ids_s[1])
    other_id = jnp.where(inst == 0, ids_s[1], ids_s[0])
    offset_id = own_id - other_id
    turn = 2.0 * jnp.pi / NINST
    own_phase = turn * own_id.astype(jnp.float32) + motion_s[1]
    other_phase = turn * other_id.astype(jnp.float32) + motion_s[1]
    angle = (jnp.pi / NINST) * offset_id.astype(jnp.float32)
    angles = jnp.where(span == 0, own_phase, jnp.where(span == 1, other_phase, angle))
    sines, cosines = jnp.sin(angles), jnp.cos(angles)

    def pick(values, k):
        return jnp.broadcast_to(values[k : k + 1], TILE)

    theta = motion_s[0] * pick(sines, 0)
    sin_theta, cos_theta = jnp.sin(theta), jnp.cos(theta)
    own_far = [heave_s[c] * pick(cosines, 0) for c in range(3)]
    other_far = [heave_s[c] * pick(cosines, 1) for c in range(3)]
    parity = 1.0 - 2.0 * lax.rem(offset_id + NINST, 2).astype(jnp.float32)
    coef = 0.5 * parity * pick(cosines, 2) / pick(sines, 2)

    @pl.when(rad > 0)
    def _():
        to_above[0].wait_recv()

    @pl.when(first)
    def _():
        for c in range(3):
            grid[c, 0] = grid[c, 1]

    step_in = length([grid[c, 1] for c in range(3)], [grid[c, 0] for c in range(3)])
    line = step_in + top[3]
    sums[place] = line
    sum_sends = [
        send(sums.at[place], sums.at[place], (sum_s, sum_r), k, device)
        for k, device in enumerate(peers)
    ]
    for copy in sum_sends:
        copy.start()

    @pl.when(rad == half)
    def _():
        walls[0].wait_recv()
        for copy in passed:
            copy.start()

    for copy in sum_sends:
        copy.wait_recv()
    own_half, lower = zero, zero
    for k in range(half):
        part = sums[k]
        own_half = own_half + part
        lower = lower + jnp.where(k < place, part, 0.0)
    cross_out[...] = own_half
    cross = send(cross_out, cross_in, one, 2, across)
    cross.start()

    @pl.when(first)
    def _():
        for c in range(2):
            wall[c] = grid[c + 1, 1]

    @pl.when((rad != 0) & (rad != half))
    def _():
        for k in range(half - 1):

            @pl.when(place == k + 1)
            def _():
                walls[k + 1].wait_recv()

    @pl.when(rad < nrad - 1)
    def _():
        to_below[0].wait_recv()

    @pl.when(last)
    def _():
        for c in range(3):
            grid[c, ROWS + 1] = grid[c, ROWS]

    step_out = length([grid[c, ROWS + 1] for c in range(3)], [grid[c, ROWS] for c in range(3)])
    wall_y, wall_z = wall[0], wall[1]
    own_wall = [
        zero,
        wall_y * cos_theta - wall_z * sin_theta - wall_y,
        wall_y * sin_theta + wall_z * cos_theta - wall_z,
    ]
    frac_out[ROWS] = own_wall[1]
    frac_out[ROWS + 1] = own_wall[2]

    cross.wait_recv()
    other_half = cross_in[...]
    inverse = 1.0 / (own_half + other_half)
    offset = lower + jnp.where(side == 1, other_half, 0.0)
    base = offset + step_in

    def displaced(frac):
        return [
            frac * own_far[0],
            (1.0 - frac) * own_wall[1] + frac * own_far[1],
            (1.0 - frac) * own_wall[2] + frac * own_far[2],
        ]

    def move(j, edge):
        frac = (base + arc[j]) * inverse
        frac_out[j] = frac
        mine = lane // 2 == j
        out = []
        for c, d in enumerate(displaced(frac)):
            disp_out[c, j] = d
            point = grid[c, j + 1] + d
            moved[c, j + 1] = point
            out.append(jnp.where(mine, pltpu.roll(point, 2 * j + 1, 1), edge[c]))
        return tuple(out)

    edges = lax.fori_loop(0, ROWS, move, (zero,) * 3, unroll=4)
    for c in range(3):
        move_edge[c] = edges[c]
    move_sends = [
        send(move_edge, move_left, one, 3, right),
        send(move_edge, move_right, one, 4, left),
    ]
    for copy in move_sends:
        copy.start()
    frac_send = send(frac_out, frac_in, one, 5, partner)
    frac_send.start()

    for c, d in enumerate(displaced(offset * inverse)):
        moved[c, 0] = grid[c, 0] + d
    for c, d in enumerate(displaced((base + top[3] + step_out) * inverse)):
        moved[c, ROWS + 1] = grid[c, ROWS + 1] + d

    @pl.when(first)
    def _():
        for c in range(3):
            moved[c, 0] = moved[c, 1]

    @pl.when(last)
    def _():
        for c in range(3):
            moved[c, ROWS + 1] = moved[c, ROWS]

    for copy in move_sends:
        copy.wait_recv()
    even = lax.rem(lane, 2) == 0
    beside = [jnp.where(even, move_left[c], move_right[c]) for c in range(3)]
    at_low, at_high = span == 0, span == 7
    span_scale = jnp.where(at_low | at_high, 1.0, 0.5)

    def slopes(j, carry):
        one_sided = (first & (j == 0)) | (last & (j == ROWS - 1))
        scale = jnp.where(one_sided, 1.0, 0.5)
        t, r, z = [], [], []
        for c in range(3):
            here = moved[c, j + 1]
            out = pltpu.roll(beside[c], lax.rem(127 - 2 * j, 128), 1)
            ahead = pltpu.roll(jnp.where(lane == 0, out, here), 127, 1)
            behind = pltpu.roll(jnp.where(lane == 127, out, here), 1, 1)
            t.append((ahead - behind) * 0.5)
            r.append((moved[c, j + 2] - moved[c, j]) * scale)
            over = jnp.where(at_high, here, pltpu.roll(here, 7, 0))
            under = jnp.where(at_low, here, pltpu.roll(here, 1, 0))
            z.append((over - under) * span_scale)
            e_t[c, j] = t[c]
            e_r[c, j] = r[c]
        vol_out[j] = (
            r[0] * (t[1] * z[2] - t[2] * z[1])
            + r[1] * (t[2] * z[0] - t[0] * z[2])
            + r[2] * (t[0] * z[1] - t[1] * z[0])
        )
        return carry

    lax.fori_loop(0, ROWS, slopes, 0, unroll=2)
    vol_send = send(vol_out, vol_in, one, 6, partner)
    vol_send.start()

    @pl.when(rad > 0)
    def _():
        to_above[1].wait_recv()

    @pl.when(first)
    def _():
        flow[:, 0:2] = jnp.zeros((5, 2, *TILE), jnp.float32)

    @pl.when(rad < nrad - 1)
    def _():
        to_below[1].wait_recv()

    @pl.when(last)
    def _():
        flow[:, ROWS + 2 : ROWS + 4] = jnp.zeros((5, 2, *TILE), jnp.float32)

    for copy in flow_sends:
        copy.wait_recv()
    loads[2].wait()
    frac_send.wait_recv()
    low = lax.rem(lane, 4) < 2
    for c in range(5):
        flow_left[c] = jnp.where(low, flow_left[c], flow_right[c])
    other_wall = [zero, frac_in[ROWS], frac_in[ROWS + 1]]
    start = [stream_s[c] - coef * other_wall[c] for c in range(3)]
    slope = [coef * (other_wall[c] - other_far[c]) for c in range(3)]

    def fluxes(j, carry):
        frac = frac_in[j]
        relative = [start[c] + frac * slope[c] for c in range(3)]
        speed_t = sum(relative[c] * e_t[c, j] for c in range(3))
        speed_r = sum(relative[c] * e_r[c, j] for c in range(3))
        rows = [[flow[c, j + k] for c in range(5)] for k in range(5)]
        here = rows[2]
        shift = lax.rem(126 - 4 * j, 128)
        out = [pltpu.roll(flow_left[c], shift, 1) for c in range(5)]
        m2 = [pltpu.roll(jnp.where(lane >= 126, out[c], here[c]), 2, 1) for c in range(5)]
        m1 = [pltpu.roll(jnp.where(lane == 127, out[c], here[c]), 1, 1) for c in range(5)]
        p1 = [pltpu.roll(jnp.where(lane == 0, out[c], here[c]), 127, 1) for c in range(5)]
        p2 = [pltpu.roll(jnp.where(lane <= 1, out[c], here[c]), 126, 1) for c in range(5)]
        term_t = jst(m2, m1, here, p1, p2, speed_t)
        term_r = jst(*rows, speed_r)
        for c in range(5):
            res_out[c, j] = term_t[c] + term_r[c] + rest_v[c, j]
        return carry

    lax.fori_loop(0, ROWS, fluxes, 0)

    vol_send.wait_recv()
    for k in range(CHUNKS):
        bulk[k].wait_recv()

        def add(j, carry):
            weight = coef * vol_in[j]
            for c in range(5):
                res_out[c, j] = res_out[c, j] + weight * state_in[c, j]
            return carry

        lax.fori_loop(k * count, (k + 1) * count, add, 0, unroll=2)

    @pl.when(rad < nrad - 1)
    def _():
        for copy in to_above:
            copy.wait_send()

    @pl.when(rad > 0)
    def _():
        for copy in to_below:
            copy.wait_send()

    @pl.when(first)
    def _():
        for copy in walls:
            copy.wait_send()

    @pl.when(rad == half)
    def _():
        for copy in passed:
            copy.wait_send()

    for copy in flow_sends + sum_sends + [cross] + move_sends + [frac_send, vol_send] + bulk:
        copy.wait_send()


def store_kernel(disp, res, disp_out, res_out, sems):
    copies = [
        pltpu.make_async_copy(disp, disp_out.at[0], sems.at[0]),
        pltpu.make_async_copy(res, res_out.at[0], sems.at[1]),
    ]
    for copy in copies:
        copy.start()
    for copy in copies:
        copy.wait()


def body(nrad, ntan, *args):
    half = nrad // 2
    f32 = jnp.float32
    vmem, hbm = pltpu.VMEM, pltpu.HBM

    def tiles(*lead):
        return pltpu.VMEM((*lead, *TILE), f32)

    dma = pltpu.SemaphoreType.DMA
    scratch = [
        tiles(3, ROWS + 2), tiles(5, ROWS + 4), tiles(5, ROWS), tiles(3, ROWS + 2), tiles(ROWS),
        tiles(ROWS + 2), tiles(ROWS + 2), tiles(3, ROWS), tiles(3, ROWS), tiles(ROWS), tiles(ROWS),
        tiles(5, ROWS), tiles(2), tiles(half), tiles(), tiles(),
        tiles(5), tiles(5), tiles(5), tiles(3), tiles(3), tiles(3),
        pltpu.SMEM((2,), jnp.int32), pltpu.SMEM((2,), f32), pltpu.SMEM((3,), f32), pltpu.SMEM((3,), f32),
        dma((7,)), dma((CHUNKS,)), dma((CHUNKS,)), dma((4,)), dma((4,)),
        dma((half,)), dma((half,)), dma((half - 1,)), dma((half - 1,)), dma((7,)), dma((7,)),
    ]
    disp, res = pl.pallas_call(
        functools.partial(step_kernel, nrad, ntan),
        out_shape=[
            jax.ShapeDtypeStruct((3, ROWS, *TILE), f32),
            jax.ShapeDtypeStruct((5, ROWS, *TILE), f32),
        ],
        in_specs=[pl.BlockSpec(memory_space=hbm)] * 7,
        out_specs=[pl.BlockSpec(memory_space=vmem)] * 2,
        scratch_shapes=scratch,
        name="deform_and_residual",
        compiler_params=pltpu.CompilerParams(
            collective_id=0, has_side_effects=True, vmem_limit_bytes=24 * 2**20
        ),
    )(*(pltpu.with_memory_space_constraint(arg, hbm) for arg in args))
    return pl.pallas_call(
        store_kernel,
        out_shape=[
            jax.ShapeDtypeStruct((1, 3, ROWS, *TILE), f32),
            jax.ShapeDtypeStruct((1, 5, ROWS, *TILE), f32),
        ],
        in_specs=[pl.BlockSpec(memory_space=vmem)] * 2,
        out_specs=[pl.BlockSpec(memory_space=hbm)] * 2,
        scratch_shapes=[dma((2,))],
        name="store_results",
    )(disp, res)


def solution(mesh):
    split = P("inst", None, "rad", None, "tan")
    return jax.shard_map(
        functools.partial(body, mesh.shape["rad"], mesh.shape["tan"]),
        mesh=mesh,
        in_specs=(split, split, split, P(), P(), P(), P()),
        out_specs=(split, split),
        check_vma=False,
    )
```

time: 156 us -> 46.1 us (0.30)
  the two profiles are of different devices: /device:TPU:6 before, /device:TPU:1 now
where the time goes in v1:
time: 46.1 us; the launch traced here: 45.4 us
  Pallas kernels  43.2 us (94%)
  local copies, waits for them, and re-layouts  1.58 us (3%)
  between operations  0.65 us (1%)
    pallas_call x1, Pallas kernels, body(): pl.pallas_call(functools.partial(step_kernel, nrad, ntan), out_shape=[jax...  41 us
    pallas_call x1, Pallas kernels, body(): pl.pallas_call(store_kernel, out_shape=[jax.ShapeDtypeStruct((1, 3, ROWS,...  2.19 us
    unnamed x4, local copies, waits for them, and re-layouts  1.58 us

profile of v1, /device:TPU:1, one launch (start us, length us, event | category | flops | bytes accessed | tf_op | source)
XLA Modules:
  0.0 45.4 jit_solution(717299960792851455)
XLA Ops:
  0.6 41.0 %deform_and_residual.1 = (f32[3,32,8,128]{3,2,1,0:T(8,128)S(1)}, f32[5,32,8,128]{3,2,1,0:T(8,128)S(1)}) custom-call(f32[1,3,32,8,128]{4,3,2,1,0:T(8,128)} %coords.1, f32[1,5,32,8,128]{4,3,2,1,0:T(8,128)} %state.1, f32[1,5,32,8,128]{4,3,2,1,0:T(8,128)} %rest.1, s32[2]{0:T(128)} %ids.1, f32[2]{0:T(128)} %motion.1, f32[3]{0:T(128)} %heave.1, f32[3]{0:T(128)} %stream.1), custom_call_target="tpu_custom_call" | custom-call | tf_op jit(solution)/shard_map/deform_and_residual/pallas_call | solution.py:472
  41.6 0.0 copy-start
  41.6 0.8 %copy-done = f32[5,32,8,128]{3,2,1,0:T(8,128)} copy-done((f32[5,32,8,128]{3,2,1,0:T(8,128)}, f32[5,32,8,128]{3,2,1,0:T(8,128)S(1)}, u32[]{:S(2)}) %copy-start) | copy-done | bytes 655384
  42.5 0.0 copy-start.1
  42.5 0.7 %copy-done.1 = f32[3,32,8,128]{3,2,1,0:T(8,128)} copy-done((f32[3,32,8,128]{3,2,1,0:T(8,128)}, f32[3,32,8,128]{3,2,1,0:T(8,128)S(1)}, u32[]{:S(2)}) %copy-start.1) | copy-done | bytes 393240
  43.2 2.2 %store_results.1 = (f32[1,3,32,8,128]{4,3,2,1,0:T(8,128)}, f32[1,5,32,8,128]{4,3,2,1,0:T(8,128)}) custom-call(f32[3,32,8,128]{3,2,1,0:T(8,128)} %copy-done.1, f32[5,32,8,128]{3,2,1,0:T(8,128)} %copy-done), custom_call_target="tpu_custom_call" | custom-call | tf_op jit(solution)/shard_map/store_results/pallas_call | solution.py:486
Async XLA Ops:
  41.6 0.8 %copy-start = (f32[5,32,8,128]{3,2,1,0:T(8,128)}, f32[5,32,8,128]{3,2,1,0:T(8,128)S(1)}, u32[]{:S(2)}) copy-start(f32[5,32,8,128]{3,2,1,0:T(8,128)S(1)} %get-tuple-element.5.res) | copy-start | bytes 1966084
  42.5 0.7 %copy-start.1 = (f32[3,32,8,128]{3,2,1,0:T(8,128)}, f32[3,32,8,128]{3,2,1,0:T(8,128)S(1)}, u32[]{:S(2)}) copy-start(f32[3,32,8,128]{3,2,1,0:T(8,128)S(1)} %get-tuple-element.4.disp) | copy-start | bytes 1179652

commit v2 on v1

--- a/solution.py
+++ b/solution.py
@@ -12,7 +12,8 @@
 COEF_FOUR = 0.05
 MESH = pl.DeviceIdType.MESH
 ROWS = 32
-CHUNKS = 4
+CHUNKS = 8
+PARTS = 4
 TILE = (8, 128)
 
 
@@ -32,20 +33,22 @@
     return jnp.sqrt(d[0] * d[0] + d[1] * d[1] + d[2] * d[2])
 
 
-def jst(m2, m1, c, p1, p2, speed):
+def each_row(body, carry):
+    for j in range(ROWS):
+        carry = body(j, carry)
+    return carry
+
+
+def jst(m2, m1, c, p1, p2):
     q_m, q_c, q_p = (1.0 + w[0] * w[0] for w in (m1, c, p1))
     outer = q_p + q_m
     sensor = COEF_TWO * jnp.abs(outer - 2.0 * q_c) / (outer + 2.0 * q_c)
     fourth = jnp.maximum(0.0, COEF_FOUR - sensor)
-    size = jnp.abs(speed)
-    half = 0.5 * speed
-    near = size * (sensor + 4.0 * fourth)
-    mid = size * (2.0 * sensor + 6.0 * fourth)
-    far = size * fourth
-    return [
-        half * (p1[k] - m1[k]) - near * (p1[k] + m1[k]) + mid * c[k] + far * (p2[k] + m2[k])
-        for k in range(5)
-    ]
+    near = sensor + 4.0 * fourth
+    mid = 2.0 * sensor + 6.0 * fourth
+    odd = [0.5 * (p1[k] - m1[k]) for k in range(5)]
+    even = [near * (p1[k] + m1[k]) - mid * c[k] - fourth * (p2[k] + m2[k]) for k in range(5)]
+    return odd, even
 
 
 def step_kernel(
@@ -53,9 +56,11 @@
     coords, state, rest, ids, motion, heave, stream,
     disp_out, res_out,
     grid, flow, rest_v, moved, arc, frac_out, frac_in, e_t, e_r, vol_out, vol_in, state_in,
-    wall, sums, cross_out, cross_in, flow_edge, flow_left, flow_right, move_edge, move_left, move_right,
+    odd_t, even_t, odd_r, even_r,
+    wall, sums, cross_out, cross_in, edge_out, edge_left, edge_right, rim_out, rim_in,
     ids_s, motion_s, heave_s, stream_s,
     local, bulk_s, bulk_r, row_s, row_r, wall_s, wall_r, sum_s, sum_r, one_s, one_r,
+    frac_s, frac_r, vol_s, vol_r, ready_right, ready_left,
 ):
     rad, tan, inst = lax.axis_index("rad"), lax.axis_index("tan"), lax.axis_index("inst")
     half = nrad // 2
@@ -79,21 +84,41 @@
         pltpu.make_async_copy(stream, stream_s, local.at[6]),
     ]
     barrier = pltpu.get_barrier_semaphore()
-    for device in [partner, left, right, across] + peers:
+
+    def greet(device):
         pl.semaphore_signal(barrier, inc=1, device_id=device, device_id_type=MESH)
 
-    @pl.when(rad == half - 1)
-    def _():
-        pl.semaphore_signal(barrier, inc=1, device_id=above, device_id_type=MESH)
-
-    @pl.when(rad == half)
-    def _():
-        pl.semaphore_signal(barrier, inc=1, device_id=below, device_id_type=MESH)
-
+    for device in [partner, across] + peers:
+        greet(device)
+    pl.when(rad == half - 1)(lambda: greet(above))
+    pl.when(rad == half)(lambda: greet(below))
+    pl.when(tan < ntan - 1)(lambda: greet(right))
+    pl.when(tan == 0)(lambda: greet(left))
     for load in loads:
         load.start()
+
+    lane = lax.broadcasted_iota(jnp.int32, TILE, 1)
+    span = lax.broadcasted_iota(jnp.int32, TILE, 0)
+    zero = jnp.zeros(TILE, jnp.float32)
+    row_of, slot = lane // 4, lax.rem(lane, 4)
+
+    loads[0].wait()
+
+    def inner(j, carry):
+        before, total = carry[:3], carry[3]
+        here = tuple(grid[c, j + 1] for c in range(3))
+        total = total + length(here, before)
+        arc[j] = total
+        return (*here, total)
+
+    arc[0] = zero
+    top = lax.fori_loop(
+        1, ROWS, inner, (*(grid[c, 1] for c in range(3)), zero), unroll=4
+    )
+
     beyond = jnp.where((rad == half - 1) | (rad == half), 1, 0)
-    pl.semaphore_wait(barrier, 4 + half - 1 + beyond)
+    higher = jnp.where(tan > 0, 1, 0) + jnp.where(tan == ntan - 1, 1, 0)
+    pl.semaphore_wait(barrier, 2 + half - 1 + beyond + higher)
 
     row = (row_s, row_r)
     to_above = [
@@ -143,42 +168,62 @@
     for copy in bulk:
         copy.start()
 
-    lane = lax.broadcasted_iota(jnp.int32, TILE, 1)
-    span = lax.broadcasted_iota(jnp.int32, TILE, 0)
-    zero = jnp.zeros(TILE, jnp.float32)
-
-    loads[0].wait()
-
-    def inner(j, carry):
-        before, total = carry[:3], carry[3]
-        here = tuple(grid[c, j + 1] for c in range(3))
-        total = total + length(here, before)
-        arc[j] = total
-        return (*here, total)
-
-    arc[0] = zero
-    top = lax.fori_loop(
-        1, ROWS, inner, (*(grid[c, 1] for c in range(3)), zero), unroll=4
-    )
+    @pl.when(tan > 0)
+    def _():
+        pl.semaphore_signal(ready_right, inc=1, device_id=left, device_id_type=MESH)
+
+    @pl.when(tan == ntan - 1)
+    def _():
+        pl.semaphore_signal(ready_left, inc=1, device_id=right, device_id_type=MESH)
 
     loads[1].wait()
 
-    def pack_flow(j, edge):
-        mine = lane // 4 == j
-        return tuple(
-            jnp.where(mine, pltpu.roll(flow[c, j + 2], 4 * j + 2, 1), edge[c]) for c in range(5)
-        )
-
-    edges = lax.fori_loop(0, ROWS, pack_flow, (zero,) * 5, unroll=4)
+    def over_tan(j, packed):
+        here = [flow[c, j + 2] for c in range(5)]
+        m2, m1, p1, p2 = ([pltpu.roll(w, k, 1) for w in here] for k in (2, 1, 127, 126))
+        odd, even = jst(m2, m1, here, p1, p2)
+        for c in range(5):
+            odd_t[c, j] = odd[c]
+            even_t[c, j] = even[c]
+        mine, shift = row_of == j, (4 * j + 2) % 128
+        tight = [
+            jnp.where(mine, pltpu.roll(here[c], shift, 1), packed[c]) for c in range(5)
+        ]
+        wide = [
+            jnp.where(mine, pltpu.roll(jnp.where(lane < 64, p2[c], m2[c]), shift, 1), packed[c + 5])
+            for c in range(5)
+        ]
+        return (*tight, *wide)
+
+    packed = each_row(over_tan, (zero,) * 10)
+    tight, wide = packed[:5], packed[5:]
     for c in range(5):
-        flow_edge[c] = edges[c]
-    one = (one_s, one_r)
-    flow_sends = [
-        send(flow_edge, flow_left, one, 0, right),
-        send(flow_edge, flow_right, one, 1, left),
-    ]
-    for copy in flow_sends:
+        edge_out[c] = tight[c]
+
+    @pl.when(rad > 0)
+    def _():
+        to_above[0].wait_recv()
+
+    @pl.when(first)
+    def _():
+        for c in range(3):
+            grid[c, 0] = grid[c, 1]
+
+    step_in = length([grid[c, 1] for c in range(3)], [grid[c, 0] for c in range(3)])
+    line = step_in + top[3]
+    sums[place] = line
+    sum_sends = [
+        send(sums.at[place], sums.at[place], (sum_s, sum_r), k, device)
+        for k, device in enumerate(peers)
+    ]
+    for copy in sum_sends:
         copy.start()
+
+    @pl.when(rad == half)
+    def _():
+        walls[0].wait_recv()
+        for copy in passed:
+            copy.start()
 
     for load in loads[3:]:
         load.wait()
@@ -202,31 +247,6 @@
     parity = 1.0 - 2.0 * lax.rem(offset_id + NINST, 2).astype(jnp.float32)
     coef = 0.5 * parity * pick(cosines, 2) / pick(sines, 2)
 
-    @pl.when(rad > 0)
-    def _():
-        to_above[0].wait_recv()
-
-    @pl.when(first)
-    def _():
-        for c in range(3):
-            grid[c, 0] = grid[c, 1]
-
-    step_in = length([grid[c, 1] for c in range(3)], [grid[c, 0] for c in range(3)])
-    line = step_in + top[3]
-    sums[place] = line
-    sum_sends = [
-        send(sums.at[place], sums.at[place], (sum_s, sum_r), k, device)
-        for k, device in enumerate(peers)
-    ]
-    for copy in sum_sends:
-        copy.start()
-
-    @pl.when(rad == half)
-    def _():
-        walls[0].wait_recv()
-        for copy in passed:
-            copy.start()
-
     for copy in sum_sends:
         copy.wait_recv()
     own_half, lower = zero, zero
@@ -235,8 +255,34 @@
         own_half = own_half + part
         lower = lower + jnp.where(k < place, part, 0.0)
     cross_out[...] = own_half
+    one = (one_s, one_r)
     cross = send(cross_out, cross_in, one, 2, across)
     cross.start()
+
+    @pl.when(rad > 0)
+    def _():
+        to_above[1].wait_recv()
+
+    @pl.when(first)
+    def _():
+        flow[:, 0:2] = jnp.zeros((5, 2, *TILE), jnp.float32)
+
+    @pl.when(rad < nrad - 1)
+    def _():
+        to_below[1].wait_recv()
+
+    @pl.when(last)
+    def _():
+        flow[:, ROWS + 2 : ROWS + 4] = jnp.zeros((5, 2, *TILE), jnp.float32)
+
+    def over_rad(j, carry):
+        odd, even = jst(*([flow[c, j + k] for c in range(5)] for k in range(5)))
+        for c in range(5):
+            odd_r[c, j] = odd[c]
+            even_r[c, j] = even[c]
+        return carry
+
+    lax.fori_loop(0, ROWS, over_rad, 0, unroll=2)
 
     @pl.when(first)
     def _():
@@ -286,26 +332,44 @@
     def move(j, edge):
         frac = (base + arc[j]) * inverse
         frac_out[j] = frac
-        mine = lane // 2 == j
+        mine, shift = row_of == j, (4 * j + 2) % 128
         out = []
         for c, d in enumerate(displaced(frac)):
             disp_out[c, j] = d
             point = grid[c, j + 1] + d
             moved[c, j + 1] = point
-            out.append(jnp.where(mine, pltpu.roll(point, 2 * j + 1, 1), edge[c]))
+            out.append(jnp.where(mine, pltpu.roll(point, shift, 1), edge[c]))
         return tuple(out)
 
-    edges = lax.fori_loop(0, ROWS, move, (zero,) * 3, unroll=4)
+    edges = each_row(move, (zero,) * 3)
+
+    def slab(src, dst, sems, k):
+        size = ROWS // PARTS
+        extra = src.shape[0] - ROWS if k == PARTS - 1 else 0
+        part = pl.ds(k * size, size + extra)
+        return send(src.at[part], dst.at[part], sems, k, partner)
+
+    frac_sends = [slab(frac_out, frac_in, (frac_s, frac_r), k) for k in range(PARTS)]
+    for copy in frac_sends:
+        copy.start()
     for c in range(3):
-        move_edge[c] = edges[c]
-    move_sends = [
-        send(move_edge, move_left, one, 3, right),
-        send(move_edge, move_right, one, 4, left),
-    ]
-    for copy in move_sends:
-        copy.start()
-    frac_send = send(frac_out, frac_in, one, 5, partner)
-    frac_send.start()
+        edge_out[5 + c] = edges[c]
+    edge_sends = [
+        send(edge_out, edge_left, one, 0, right),
+        send(edge_out, edge_right, one, 1, left),
+    ]
+
+    @pl.when(tan < ntan - 1)
+    def _():
+        pl.semaphore_wait(ready_right, 1)
+
+    edge_sends[0].start()
+
+    @pl.when(tan == 0)
+    def _():
+        pl.semaphore_wait(ready_left, 1)
+
+    edge_sends[1].start()
 
     for c, d in enumerate(displaced(offset * inverse)):
         moved[c, 0] = grid[c, 0] + d
@@ -322,99 +386,98 @@
         for c in range(3):
             moved[c, ROWS + 1] = moved[c, ROWS]
 
-    for copy in move_sends:
-        copy.wait_recv()
-    even = lax.rem(lane, 2) == 0
-    beside = [jnp.where(even, move_left[c], move_right[c]) for c in range(3)]
     at_low, at_high = span == 0, span == 7
     span_scale = jnp.where(at_low | at_high, 1.0, 0.5)
 
-    def slopes(j, carry):
-        one_sided = (first & (j == 0)) | (last & (j == ROWS - 1))
-        scale = jnp.where(one_sided, 1.0, 0.5)
+    def slopes(j, packed):
+        outer = first if j == 0 else last if j == ROWS - 1 else False
+        scale = jnp.where(outer, 1.0, 0.5)
         t, r, z = [], [], []
         for c in range(3):
             here = moved[c, j + 1]
-            out = pltpu.roll(beside[c], lax.rem(127 - 2 * j, 128), 1)
-            ahead = pltpu.roll(jnp.where(lane == 0, out, here), 127, 1)
-            behind = pltpu.roll(jnp.where(lane == 127, out, here), 1, 1)
-            t.append((ahead - behind) * 0.5)
+            t.append((pltpu.roll(here, 127, 1) - pltpu.roll(here, 1, 1)) * 0.5)
             r.append((moved[c, j + 2] - moved[c, j]) * scale)
             over = jnp.where(at_high, here, pltpu.roll(here, 7, 0))
             under = jnp.where(at_low, here, pltpu.roll(here, 1, 0))
             z.append((over - under) * span_scale)
             e_t[c, j] = t[c]
             e_r[c, j] = r[c]
-        vol_out[j] = (
-            r[0] * (t[1] * z[2] - t[2] * z[1])
-            + r[1] * (t[2] * z[0] - t[0] * z[2])
-            + r[2] * (t[0] * z[1] - t[1] * z[0])
+        face = [
+            z[1] * r[2] - z[2] * r[1],
+            z[2] * r[0] - z[0] * r[2],
+            z[0] * r[1] - z[1] * r[0],
+        ]
+        vol_out[j] = t[0] * face[0] + t[1] * face[1] + t[2] * face[2]
+        mine, shift = row_of == j, (4 * j + 2) % 128
+        return tuple(
+            jnp.where(mine, pltpu.roll(face[c], shift, 1), packed[c]) for c in range(3)
         )
-        return carry
-
-    lax.fori_loop(0, ROWS, slopes, 0, unroll=2)
-    vol_send = send(vol_out, vol_in, one, 6, partner)
-    vol_send.start()
-
-    @pl.when(rad > 0)
-    def _():
-        to_above[1].wait_recv()
-
-    @pl.when(first)
-    def _():
-        flow[:, 0:2] = jnp.zeros((5, 2, *TILE), jnp.float32)
-
-    @pl.when(rad < nrad - 1)
-    def _():
-        to_below[1].wait_recv()
-
-    @pl.when(last)
-    def _():
-        flow[:, ROWS + 2 : ROWS + 4] = jnp.zeros((5, 2, *TILE), jnp.float32)
-
-    for copy in flow_sends:
+
+    face = each_row(slopes, (zero,) * 3)
+    vol_sends = [slab(vol_out, vol_in, (vol_s, vol_r), k) for k in range(PARTS)]
+    for copy in vol_sends:
+        copy.start()
+
+    for copy in edge_sends:
         copy.wait_recv()
+    beside = [jnp.where(slot < 2, edge_left[c], edge_right[c]) for c in range(8)]
+    rim = []
+    for c in range(3):
+        ahead = pltpu.roll(jnp.where(slot == 2, beside[5 + c], edges[c]), 127, 1)
+        behind = pltpu.roll(jnp.where(slot == 1, beside[5 + c], edges[c]), 1, 1)
+        rim.append((ahead - behind) * 0.5)
+    rim_out[...] = rim[0] * face[0] + rim[1] * face[1] + rim[2] * face[2]
+    rim_send = send(rim_out, rim_in, one, 3, partner)
+    rim_send.start()
+    m1, p1, m2, p2 = [], [], [], []
+    for c in range(5):
+        m2.append(jnp.where(slot < 2, wide[c], pltpu.roll(beside[c], 2, 1)))
+        p2.append(jnp.where(slot < 2, pltpu.roll(beside[c], 126, 1), wide[c]))
+        near = pltpu.roll(jnp.where(slot == 1, beside[c], tight[c]), 1, 1)
+        m1.append(jnp.where(slot == 0, pltpu.roll(wide[c], 127, 1), near))
+        near = pltpu.roll(jnp.where(slot == 2, beside[c], tight[c]), 127, 1)
+        p1.append(jnp.where(slot == 3, pltpu.roll(wide[c], 1, 1), near))
+    rim_odd, rim_even = jst(m2, m1, tight, p1, p2)
+
     loads[2].wait()
-    frac_send.wait_recv()
-    low = lax.rem(lane, 4) < 2
-    for c in range(5):
-        flow_left[c] = jnp.where(low, flow_left[c], flow_right[c])
+    for copy in frac_sends:
+        copy.wait_recv()
     other_wall = [zero, frac_in[ROWS], frac_in[ROWS + 1]]
     start = [stream_s[c] - coef * other_wall[c] for c in range(3)]
     slope = [coef * (other_wall[c] - other_far[c]) for c in range(3)]
+    outer_two = (lane < 2) | (lane > 125)
+    outer_one = (lane == 0) | (lane == 127)
 
     def fluxes(j, carry):
+        shift = (126 - 4 * j) % 128
         frac = frac_in[j]
         relative = [start[c] + frac * slope[c] for c in range(3)]
-        speed_t = sum(relative[c] * e_t[c, j] for c in range(3))
+        tangent = [jnp.where(outer_one, pltpu.roll(rim[c], shift, 1), e_t[c, j]) for c in range(3)]
+        speed_t = sum(relative[c] * tangent[c] for c in range(3))
         speed_r = sum(relative[c] * e_r[c, j] for c in range(3))
-        rows = [[flow[c, j + k] for c in range(5)] for k in range(5)]
-        here = rows[2]
-        shift = lax.rem(126 - 4 * j, 128)
-        out = [pltpu.roll(flow_left[c], shift, 1) for c in range(5)]
-        m2 = [pltpu.roll(jnp.where(lane >= 126, out[c], here[c]), 2, 1) for c in range(5)]
-        m1 = [pltpu.roll(jnp.where(lane == 127, out[c], here[c]), 1, 1) for c in range(5)]
-        p1 = [pltpu.roll(jnp.where(lane == 0, out[c], here[c]), 127, 1) for c in range(5)]
-        p2 = [pltpu.roll(jnp.where(lane <= 1, out[c], here[c]), 126, 1) for c in range(5)]
-        term_t = jst(m2, m1, here, p1, p2, speed_t)
-        term_r = jst(*rows, speed_r)
+        size_t, size_r = jnp.abs(speed_t), jnp.abs(speed_r)
         for c in range(5):
-            res_out[c, j] = term_t[c] + term_r[c] + rest_v[c, j]
+            odd = jnp.where(outer_two, pltpu.roll(rim_odd[c], shift, 1), odd_t[c, j])
+            even = jnp.where(outer_two, pltpu.roll(rim_even[c], shift, 1), even_t[c, j])
+            over_t = speed_t * odd - size_t * even
+            over_r = speed_r * odd_r[c, j] - size_r * even_r[c, j]
+            res_out[c, j] = over_t + over_r + rest_v[c, j]
         return carry
 
-    lax.fori_loop(0, ROWS, fluxes, 0)
-
-    vol_send.wait_recv()
-    for k in range(CHUNKS):
-        bulk[k].wait_recv()
-
-        def add(j, carry):
-            weight = coef * vol_in[j]
-            for c in range(5):
-                res_out[c, j] = res_out[c, j] + weight * state_in[c, j]
-            return carry
-
-        lax.fori_loop(k * count, (k + 1) * count, add, 0, unroll=2)
+    each_row(fluxes, 0)
+
+    for copy in bulk + vol_sends + [rim_send]:
+        copy.wait_recv()
+    rim_vol = rim_in[...]
+
+    def add(j, carry):
+        shift = (126 - 4 * j) % 128
+        weight = coef * jnp.where(outer_one, pltpu.roll(rim_vol, shift, 1), vol_in[j])
+        for c in range(5):
+            res_out[c, j] = res_out[c, j] + weight * state_in[c, j]
+        return carry
+
+    each_row(add, 0)
 
     @pl.when(rad < nrad - 1)
     def _():
@@ -436,7 +499,7 @@
         for copy in passed:
             copy.wait_send()
 
-    for copy in flow_sends + sum_sends + [cross] + move_sends + [frac_send, vol_send] + bulk:
+    for copy in sum_sends + [cross, rim_send] + edge_sends + frac_sends + vol_sends + bulk:
         copy.wait_send()
 
 
@@ -463,11 +526,13 @@
     scratch = [
         tiles(3, ROWS + 2), tiles(5, ROWS + 4), tiles(5, ROWS), tiles(3, ROWS + 2), tiles(ROWS),
         tiles(ROWS + 2), tiles(ROWS + 2), tiles(3, ROWS), tiles(3, ROWS), tiles(ROWS), tiles(ROWS),
-        tiles(5, ROWS), tiles(2), tiles(half), tiles(), tiles(),
-        tiles(5), tiles(5), tiles(5), tiles(3), tiles(3), tiles(3),
+        tiles(5, ROWS), tiles(5, ROWS), tiles(5, ROWS), tiles(5, ROWS), tiles(5, ROWS),
+        tiles(2), tiles(half), tiles(), tiles(), tiles(8), tiles(8), tiles(8), tiles(), tiles(),
         pltpu.SMEM((2,), jnp.int32), pltpu.SMEM((2,), f32), pltpu.SMEM((3,), f32), pltpu.SMEM((3,), f32),
         dma((7,)), dma((CHUNKS,)), dma((CHUNKS,)), dma((4,)), dma((4,)),
-        dma((half,)), dma((half,)), dma((half - 1,)), dma((half - 1,)), dma((7,)), dma((7,)),
+        dma((half,)), dma((half,)), dma((half - 1,)), dma((half - 1,)), dma((4,)), dma((4,)),
+        dma((PARTS,)), dma((PARTS,)), dma((PARTS,)), dma((PARTS,)),
+        pltpu.SemaphoreType.REGULAR, pltpu.SemaphoreType.REGULAR,
     ]
     disp, res = pl.pallas_call(
         functools.partial(step_kernel, nrad, ntan),
@@ -493,7 +558,7 @@
         out_specs=[pl.BlockSpec(memory_space=hbm)] * 2,
         scratch_shapes=[dma((2,))],
         name="store_results",
-    )(disp, res)
+    )(*(pltpu.with_memory_space_constraint(x, vmem) for x in (disp, res)))
 
 
 def solution(mesh):

time: 46.1 us -> 38.6 us (0.84)
  Pallas kernels: 43.2 us -> 37.5 us
  local copies, waits for them, and re-layouts: 1.58 us -> 0 us
    pallas_call x1, Pallas kernels: 41 us -> 36.5 us  [body(): pl.pallas_call(functools.partial(step_kernel, nrad, ntan), out_shape=[jax...]
    unnamed x4 -> x0, local copies, waits for them, and re-layouts: 1.58 us -> none
    pallas_call x1, Pallas kernels: 2.19 us -> 0.99 us  [body(): pl.pallas_call(store_kernel, out_shape=[jax.ShapeDtypeStruct((1, 3, ROWS,...]
where the time goes in v2:
time: 38.6 us; the launch traced here: 38.1 us
  Pallas kernels  37.5 us (97%)
  between operations  0.64 us (2%)
    pallas_call x1, Pallas kernels, body(): pl.pallas_call(functools.partial(step_kernel, nrad, ntan), out_shape=[jax...  36.5 us
    pallas_call x1, Pallas kernels, body(): pl.pallas_call(store_kernel, out_shape=[jax.ShapeDtypeStruct((1, 3, ROWS,...  0.99 us

profile of v2, /device:TPU:1, one launch (start us, length us, event | category | flops | bytes accessed | tf_op | source)
XLA Modules:
  0.0 38.1 jit_solution(13618591914346253531)
XLA Ops:
  0.6 36.5 %deform_and_residual.1 = (f32[3,32,8,128]{3,2,1,0:T(8,128)S(1)}, f32[5,32,8,128]{3,2,1,0:T(8,128)S(1)}) custom-call(f32[1,3,32,8,128]{4,3,2,1,0:T(8,128)} %coords.1, f32[1,5,32,8,128]{4,3,2,1,0:T(8,128)} %state.1, f32[1,5,32,8,128]{4,3,2,1,0:T(8,128)} %rest.1, s32[2]{0:T(128)} %ids.1, f32[2]{0:T(128)} %motion.1, f32[3]{0:T(128)} %heave.1, f32[3]{0:T(128)} %stream.1), custom_call_target="tpu_custom_call" | custom-call | tf_op jit(solution)/shard_map/deform_and_residual/pallas_call | solution.py:537
  37.1 1.0 %store_results.1 = (f32[1,3,32,8,128]{4,3,2,1,0:T(8,128)}, f32[1,5,32,8,128]{4,3,2,1,0:T(8,128)}) custom-call(f32[3,32,8,128]{3,2,1,0:T(8,128)S(1)} %get-tuple-element.4.disp, f32[5,32,8,128]{3,2,1,0:T(8,128)S(1)} %get-tuple-element.5.res), custom_call_target="tpu_custom_call" | custom-call | tf_op jit(solution)/shard_map/store_results/pallas_call | solution.py:551

commit v3 on v2

--- a/solution.py
+++ b/solution.py
@@ -57,7 +57,7 @@
     disp_out, res_out,
     grid, flow, rest_v, moved, arc, frac_out, frac_in, e_t, e_r, vol_out, vol_in, state_in,
     odd_t, even_t, odd_r, even_r,
-    wall, sums, cross_out, cross_in, edge_out, edge_left, edge_right, rim_out, rim_in,
+    wall, sums, far_out, far_in, far_prior, edge_out, edge_left, edge_right, rim_out, rim_in,
     ids_s, motion_s, heave_s, stream_s,
     local, bulk_s, bulk_r, row_s, row_r, wall_s, wall_r, sum_s, sum_r, one_s, one_r,
     frac_s, frac_r, vol_s, vol_r, ready_right, ready_left,
@@ -120,6 +120,13 @@
     higher = jnp.where(tan > 0, 1, 0) + jnp.where(tan == ntan - 1, 1, 0)
     pl.semaphore_wait(barrier, 2 + half - 1 + beyond + higher)
 
+    for c in range(3):
+        far_out[c] = grid[c, 1]
+        far_out[3 + c] = grid[c, ROWS]
+    far_out[6] = top[3]
+    one = (one_s, one_r)
+    far = send(far_out, far_in, one, 2, across)
+    far_last = send(far_in.at[pl.ds(3, 3)], far_prior, one, 4, above)
     row = (row_s, row_r)
     to_above = [
         send(coords.at[0, :, ROWS - 1], grid.at[:, 0], row, 0, above),
@@ -144,6 +151,8 @@
         for k in range(CHUNKS)
     ]
 
+    far.start()
+
     @pl.when(rad < nrad - 1)
     def _():
         to_above[0].start()
@@ -175,6 +184,58 @@
     @pl.when(tan == ntan - 1)
     def _():
         pl.semaphore_signal(ready_left, inc=1, device_id=right, device_id_type=MESH)
+
+    far.wait_recv()
+
+    @pl.when(place < half - 1)
+    def _():
+        far_last.start()
+
+    @pl.when(rad > 0)
+    def _():
+        to_above[0].wait_recv()
+
+    @pl.when(first)
+    def _():
+        for c in range(3):
+            grid[c, 0] = grid[c, 1]
+
+    @pl.when(rad < nrad - 1)
+    def _():
+        to_below[0].wait_recv()
+
+    @pl.when(last)
+    def _():
+        for c in range(3):
+            grid[c, ROWS + 1] = grid[c, ROWS]
+
+    step_in = length([grid[c, 1] for c in range(3)], [grid[c, 0] for c in range(3)])
+    step_out = length([grid[c, ROWS + 1] for c in range(3)], [grid[c, ROWS] for c in range(3)])
+
+    @pl.when(place > 0)
+    def _():
+        far_last.wait_recv()
+
+    @pl.when(place == 0)
+    def _():
+        for c in range(3):
+            far_prior[c] = far_in[c]
+
+    far_step = length([far_in[c] for c in range(3)], [far_prior[c] for c in range(3)])
+    sums[place, 0] = step_in + top[3]
+    sums[place, 1] = far_in[6] + far_step + jnp.where(rad == half - 1, step_out, 0.0)
+    sum_sends = [
+        send(sums.at[place], sums.at[place], (sum_s, sum_r), k, device)
+        for k, device in enumerate(peers)
+    ]
+    for copy in sum_sends:
+        copy.start()
+
+    @pl.when(rad == half)
+    def _():
+        walls[0].wait_recv()
+        for copy in passed:
+            copy.start()
 
     loads[1].wait()
 
@@ -200,31 +261,6 @@
     for c in range(5):
         edge_out[c] = tight[c]
 
-    @pl.when(rad > 0)
-    def _():
-        to_above[0].wait_recv()
-
-    @pl.when(first)
-    def _():
-        for c in range(3):
-            grid[c, 0] = grid[c, 1]
-
-    step_in = length([grid[c, 1] for c in range(3)], [grid[c, 0] for c in range(3)])
-    line = step_in + top[3]
-    sums[place] = line
-    sum_sends = [
-        send(sums.at[place], sums.at[place], (sum_s, sum_r), k, device)
-        for k, device in enumerate(peers)
-    ]
-    for copy in sum_sends:
-        copy.start()
-
-    @pl.when(rad == half)
-    def _():
-        walls[0].wait_recv()
-        for copy in passed:
-            copy.start()
-
     for load in loads[3:]:
         load.wait()
     own_id = jnp.where(inst == 0, ids_s[0], ids_s[1])
@@ -249,40 +285,11 @@
 
     for copy in sum_sends:
         copy.wait_recv()
-    own_half, lower = zero, zero
+    own_half, other_half, lower = zero, zero, zero
     for k in range(half):
-        part = sums[k]
-        own_half = own_half + part
-        lower = lower + jnp.where(k < place, part, 0.0)
-    cross_out[...] = own_half
-    one = (one_s, one_r)
-    cross = send(cross_out, cross_in, one, 2, across)
-    cross.start()
-
-    @pl.when(rad > 0)
-    def _():
-        to_above[1].wait_recv()
-
-    @pl.when(first)
-    def _():
-        flow[:, 0:2] = jnp.zeros((5, 2, *TILE), jnp.float32)
-
-    @pl.when(rad < nrad - 1)
-    def _():
-        to_below[1].wait_recv()
-
-    @pl.when(last)
-    def _():
-        flow[:, ROWS + 2 : ROWS + 4] = jnp.zeros((5, 2, *TILE), jnp.float32)
-
-    def over_rad(j, carry):
-        odd, even = jst(*([flow[c, j + k] for c in range(5)] for k in range(5)))
-        for c in range(5):
-            odd_r[c, j] = odd[c]
-            even_r[c, j] = even[c]
-        return carry
-
-    lax.fori_loop(0, ROWS, over_rad, 0, unroll=2)
+        own_half = own_half + sums[k, 0]
+        other_half = other_half + sums[k, 1]
+        lower = lower + jnp.where(k < place, sums[k, 0], 0.0)
 
     @pl.when(first)
     def _():
@@ -297,16 +304,6 @@
             def _():
                 walls[k + 1].wait_recv()
 
-    @pl.when(rad < nrad - 1)
-    def _():
-        to_below[0].wait_recv()
-
-    @pl.when(last)
-    def _():
-        for c in range(3):
-            grid[c, ROWS + 1] = grid[c, ROWS]
-
-    step_out = length([grid[c, ROWS + 1] for c in range(3)], [grid[c, ROWS] for c in range(3)])
     wall_y, wall_z = wall[0], wall[1]
     own_wall = [
         zero,
@@ -316,8 +313,6 @@
     frac_out[ROWS] = own_wall[1]
     frac_out[ROWS + 1] = own_wall[2]
 
-    cross.wait_recv()
-    other_half = cross_in[...]
     inverse = 1.0 / (own_half + other_half)
     offset = lower + jnp.where(side == 1, other_half, 0.0)
     base = offset + step_in
@@ -418,6 +413,31 @@
     for copy in vol_sends:
         copy.start()
 
+    @pl.when(rad > 0)
+    def _():
+        to_above[1].wait_recv()
+
+    @pl.when(first)
+    def _():
+        flow[:, 0:2] = jnp.zeros((5, 2, *TILE), jnp.float32)
+
+    @pl.when(rad < nrad - 1)
+    def _():
+        to_below[1].wait_recv()
+
+    @pl.when(last)
+    def _():
+        flow[:, ROWS + 2 : ROWS + 4] = jnp.zeros((5, 2, *TILE), jnp.float32)
+
+    def over_rad(j, carry):
+        odd, even = jst(*([flow[c, j + k] for c in range(5)] for k in range(5)))
+        for c in range(5):
+            odd_r[c, j] = odd[c]
+            even_r[c, j] = even[c]
+        return carry
+
+    lax.fori_loop(0, ROWS, over_rad, 0, unroll=2)
+
     for copy in edge_sends:
         copy.wait_recv()
     beside = [jnp.where(slot < 2, edge_left[c], edge_right[c]) for c in range(8)]
@@ -466,18 +486,16 @@
 
     each_row(fluxes, 0)
 
-    for copy in bulk + vol_sends + [rim_send]:
-        copy.wait_recv()
+    rim_send.wait_recv()
     rim_vol = rim_in[...]
-
-    def add(j, carry):
-        shift = (126 - 4 * j) % 128
-        weight = coef * jnp.where(outer_one, pltpu.roll(rim_vol, shift, 1), vol_in[j])
-        for c in range(5):
-            res_out[c, j] = res_out[c, j] + weight * state_in[c, j]
-        return carry
-
-    each_row(add, 0)
+    for k in range(PARTS):
+        for copy in bulk[k * CHUNKS // PARTS : (k + 1) * CHUNKS // PARTS] + [vol_sends[k]]:
+            copy.wait_recv()
+        for j in range(k * ROWS // PARTS, (k + 1) * ROWS // PARTS):
+            shift = (126 - 4 * j) % 128
+            weight = coef * jnp.where(outer_one, pltpu.roll(rim_vol, shift, 1), vol_in[j])
+            for c in range(5):
+                res_out[c, j] = res_out[c, j] + weight * state_in[c, j]
 
     @pl.when(rad < nrad - 1)
     def _():
@@ -499,7 +517,11 @@
         for copy in passed:
             copy.wait_send()
 
-    for copy in sum_sends + [cross, rim_send] + edge_sends + frac_sends + vol_sends + bulk:
+    @pl.when(place < half - 1)
+    def _():
+        far_last.wait_send()
+
+    for copy in sum_sends + [far, rim_send] + edge_sends + frac_sends + vol_sends + bulk:
         copy.wait_send()
 
 
@@ -527,10 +549,10 @@
         tiles(3, ROWS + 2), tiles(5, ROWS + 4), tiles(5, ROWS), tiles(3, ROWS + 2), tiles(ROWS),
         tiles(ROWS + 2), tiles(ROWS + 2), tiles(3, ROWS), tiles(3, ROWS), tiles(ROWS), tiles(ROWS),
         tiles(5, ROWS), tiles(5, ROWS), tiles(5, ROWS), tiles(5, ROWS), tiles(5, ROWS),
-        tiles(2), tiles(half), tiles(), tiles(), tiles(8), tiles(8), tiles(8), tiles(), tiles(),
+        tiles(2), tiles(half, 2), tiles(7), tiles(7), tiles(3), tiles(8), tiles(8), tiles(8), tiles(), tiles(),
         pltpu.SMEM((2,), jnp.int32), pltpu.SMEM((2,), f32), pltpu.SMEM((3,), f32), pltpu.SMEM((3,), f32),
         dma((7,)), dma((CHUNKS,)), dma((CHUNKS,)), dma((4,)), dma((4,)),
-        dma((half,)), dma((half,)), dma((half - 1,)), dma((half - 1,)), dma((4,)), dma((4,)),
+        dma((half,)), dma((half,)), dma((half - 1,)), dma((half - 1,)), dma((5,)), dma((5,)),
         dma((PARTS,)), dma((PARTS,)), dma((PARTS,)), dma((PARTS,)),
         pltpu.SemaphoreType.REGULAR, pltpu.SemaphoreType.REGULAR,
     ]

time: 38.6 us -> 32.2 us (0.83)
  the two profiles are of different devices: /device:TPU:1 before, /device:TPU:29 now
where the time goes in v3:
time: 32.2 us; the launch traced here: 32 us
  Pallas kernels  31.4 us (98%)
  between operations  0.64 us (2%)
    pallas_call x1, Pallas kernels, body(): pl.pallas_call(functools.partial(step_kernel, nrad, ntan), out_shape=[jax...  30.4 us
    pallas_call x1, Pallas kernels, body(): pl.pallas_call(store_kernel, out_shape=[jax.ShapeDtypeStruct((1, 3, ROWS,...  0.99 us

profile of v3, /device:TPU:29, one launch (start us, length us, event | category | flops | bytes accessed | tf_op | source)
XLA Modules:
  0.0 32.0 jit_solution(8025024289507419208)
XLA Ops:
  0.6 30.4 %deform_and_residual.1 = (f32[3,32,8,128]{3,2,1,0:T(8,128)S(1)}, f32[5,32,8,128]{3,2,1,0:T(8,128)S(1)}) custom-call(f32[1,3,32,8,128]{4,3,2,1,0:T(8,128)} %coords.1, f32[1,5,32,8,128]{4,3,2,1,0:T(8,128)} %state.1, f32[1,5,32,8,128]{4,3,2,1,0:T(8,128)} %rest.1, s32[2]{0:T(128)} %ids.1, f32[2]{0:T(128)} %motion.1, f32[3]{0:T(128)} %heave.1, f32[3]{0:T(128)} %stream.1), custom_call_target="tpu_custom_call" | custom-call | tf_op jit(solution)/shard_map/deform_and_residual/pallas_call | solution.py:559
  31.0 1.0 %store_results.1 = (f32[1,3,32,8,128]{4,3,2,1,0:T(8,128)}, f32[1,5,32,8,128]{4,3,2,1,0:T(8,128)}) custom-call(f32[3,32,8,128]{3,2,1,0:T(8,128)S(1)} %get-tuple-element.4.disp, f32[5,32,8,128]{3,2,1,0:T(8,128)S(1)} %get-tuple-element.5.res), custom_call_target="tpu_custom_call" | custom-call | tf_op jit(solution)/shard_map/store_results/pallas_call | solution.py:573

commit v4 on v3

--- a/solution.py
+++ b/solution.py
@@ -12,7 +12,9 @@
 COEF_FOUR = 0.05
 MESH = pl.DeviceIdType.MESH
 ROWS = 32
-CHUNKS = 8
+RAW = 24
+CUTS = (0, 2, 8, 14, 20, RAW)
+AHEAD = 3
 PARTS = 4
 TILE = (8, 128)
 
@@ -55,12 +57,12 @@
     nrad, ntan,
     coords, state, rest, ids, motion, heave, stream,
     disp_out, res_out,
-    grid, flow, rest_v, moved, arc, frac_out, frac_in, e_t, e_r, vol_out, vol_in, state_in,
+    grid, flow, rest_v, moved, arc, frac_out, frac_in, e_t, e_r, vol_out, vol_in, product_out, state_in,
     odd_t, even_t, odd_r, even_r,
     wall, sums, far_out, far_in, far_prior, edge_out, edge_left, edge_right, rim_out, rim_in,
     ids_s, motion_s, heave_s, stream_s,
     local, bulk_s, bulk_r, row_s, row_r, wall_s, wall_r, sum_s, sum_r, one_s, one_r,
-    frac_s, frac_r, vol_s, vol_r, ready_right, ready_left,
+    frac_s, frac_r, vol_s, vol_r, ready_rad, ready_next, ready_right, ready_left,
 ):
     rad, tan, inst = lax.axis_index("rad"), lax.axis_index("tan"), lax.axis_index("inst")
     half = nrad // 2
@@ -84,16 +86,22 @@
         pltpu.make_async_copy(stream, stream_s, local.at[6]),
     ]
     barrier = pltpu.get_barrier_semaphore()
-
-    def greet(device):
-        pl.semaphore_signal(barrier, inc=1, device_id=device, device_id_type=MESH)
-
-    for device in [partner, across] + peers:
-        greet(device)
-    pl.when(rad == half - 1)(lambda: greet(above))
-    pl.when(rad == half)(lambda: greet(below))
-    pl.when(tan < ntan - 1)(lambda: greet(right))
-    pl.when(tan == 0)(lambda: greet(left))
+    turned = tan == 0
+
+    def signal(semaphore, device, condition=None):
+        def run():
+            pl.semaphore_signal(semaphore, inc=1, device_id=device, device_id_type=MESH)
+
+        run() if condition is None else pl.when(condition)(run)
+
+    signal(barrier, partner)
+    signal(barrier, across)
+    for k, device in enumerate(peers):
+        lower = place + k + 1 >= half
+        signal(barrier, device, (lower & turned) | jnp.logical_not(lower | turned))
+    signal(barrier, below, rad == half)
+    signal(barrier, right, tan < ntan - 1)
+    signal(barrier, left, turned)
     for load in loads:
         load.start()
 
@@ -101,6 +109,49 @@
     span = lax.broadcasted_iota(jnp.int32, TILE, 0)
     zero = jnp.zeros(TILE, jnp.float32)
     row_of, slot = lane // 4, lax.rem(lane, 4)
+
+    awaited = jnp.where(turned, half - 1 - place, place)
+    higher = jnp.where(tan > 0, 1, 0) + jnp.where(tan == ntan - 1, 1, 0)
+    pl.semaphore_wait(barrier, 2 + awaited + jnp.where(rad == half - 1, 1, 0) + higher)
+    for k, device in enumerate(peers):
+        lower = place + k + 1 >= half
+        signal(ready_rad, device, (lower & jnp.logical_not(turned)) | (turned & jnp.logical_not(lower)))
+    signal(ready_next, above, rad == half - 1)
+    signal(ready_right, left, tan > 0)
+    signal(ready_left, right, tan == ntan - 1)
+
+    one = (one_s, one_r)
+    far = send(far_out, far_in, one, 2, across)
+    far_last = send(far_in.at[pl.ds(3, 3)], far_prior, one, 4, above)
+    near_last = send(coords.at[0, :, ROWS - 1], far_prior, one, 4, peers[0])
+    row = (row_s, row_r)
+    to_above = [
+        send(coords.at[0, :, ROWS - 1], grid.at[:, 0], row, 0, above),
+        send(state.at[0, :, pl.ds(ROWS - 2, 2)], flow.at[:, pl.ds(0, 2)], row, 1, above),
+    ]
+    to_below = [
+        send(coords.at[0, :, 0], grid.at[:, ROWS + 1], row, 2, below),
+        send(state.at[0, :, pl.ds(0, 2)], flow.at[:, pl.ds(ROWS + 2, 2)], row, 3, below),
+    ]
+    far_first = send(far_in.at[pl.ds(0, 3)], grid.at[:, ROWS + 1], row, 2, peers[-1])
+    walls = [
+        send(coords.at[0, pl.ds(1, 2), 0], wall, (wall_s, wall_r), k, device)
+        for k, device in enumerate([across] + peers)
+    ]
+    passed = [send(wall, wall, (wall_s, wall_r), k + 1, device) for k, device in enumerate(peers)]
+    bulk = [
+        send(
+            state.at[0, :, pl.ds(low, high - low)],
+            state_in.at[:, pl.ds(low, high - low)],
+            (bulk_s, bulk_r), k, partner,
+        )
+        for k, (low, high) in enumerate(zip(CUTS, CUTS[1:]))
+    ]
+
+    pl.when(turned & (place < half - 1))(to_above[0].start)
+    bulk[0].start()
+    pl.when(rad == half - 1)(to_above[0].start)
+    pl.when(first)(walls[0].start)
 
     loads[0].wait()
 
@@ -116,80 +167,46 @@
         1, ROWS, inner, (*(grid[c, 1] for c in range(3)), zero), unroll=4
     )
 
-    beyond = jnp.where((rad == half - 1) | (rad == half), 1, 0)
-    higher = jnp.where(tan > 0, 1, 0) + jnp.where(tan == ntan - 1, 1, 0)
-    pl.semaphore_wait(barrier, 2 + half - 1 + beyond + higher)
-
     for c in range(3):
         far_out[c] = grid[c, 1]
         far_out[3 + c] = grid[c, ROWS]
     far_out[6] = top[3]
-    one = (one_s, one_r)
-    far = send(far_out, far_in, one, 2, across)
-    far_last = send(far_in.at[pl.ds(3, 3)], far_prior, one, 4, above)
-    row = (row_s, row_r)
-    to_above = [
-        send(coords.at[0, :, ROWS - 1], grid.at[:, 0], row, 0, above),
-        send(state.at[0, :, pl.ds(ROWS - 2, 2)], flow.at[:, pl.ds(0, 2)], row, 1, above),
-    ]
-    to_below = [
-        send(coords.at[0, :, 0], grid.at[:, ROWS + 1], row, 2, below),
-        send(state.at[0, :, pl.ds(0, 2)], flow.at[:, pl.ds(ROWS + 2, 2)], row, 3, below),
-    ]
-    walls = [
-        send(coords.at[0, pl.ds(1, 2), 0], wall, (wall_s, wall_r), k, device)
-        for k, device in enumerate([across] + peers)
-    ]
-    passed = [send(wall, wall, (wall_s, wall_r), k + 1, device) for k, device in enumerate(peers)]
-    count = ROWS // CHUNKS
-    bulk = [
-        send(
-            state.at[0, :, pl.ds(k * count, count)],
-            state_in.at[:, pl.ds(k * count, count)],
-            (bulk_s, bulk_r), k, partner,
-        )
-        for k in range(CHUNKS)
-    ]
-
     far.start()
-
-    @pl.when(rad < nrad - 1)
-    def _():
-        to_above[0].start()
-
-    @pl.when(rad > 0)
-    def _():
-        to_below[0].start()
+    pl.when(rad == half - 1)(to_above[1].start)
+    for copy in bulk[1:AHEAD]:
+        copy.start()
+
+    @pl.when(turned)
+    def _():
+        for copy in bulk[AHEAD:]:
+            copy.start()
+
+    pl.when(awaited < half - 1)(
+        lambda: pl.semaphore_wait(ready_rad, half - 1 - awaited)
+    )
+
+    pl.when((place < half - 1) & jnp.logical_not(turned))(to_above[0].start)
+    pl.when(place < half - 1)(to_above[1].start)
+    pl.when(rad == half - 1)(near_last.start)
 
     @pl.when(first)
     def _():
-        for copy in walls:
+        for copy in walls[1:]:
             copy.start()
 
-    @pl.when(rad < nrad - 1)
-    def _():
-        to_above[1].start()
-
-    @pl.when(rad > 0)
-    def _():
+    @pl.when(place > 0)
+    def _():
+        for copy in to_below:
+            copy.start()
+
+    far.wait_recv()
+    pl.when(place < half - 1)(far_last.start)
+    pl.when(first)(far_first.start)
+
+    @pl.when(rad == half)
+    def _():
+        pl.semaphore_wait(ready_next, 1)
         to_below[1].start()
-
-    for copy in bulk:
-        copy.start()
-
-    @pl.when(tan > 0)
-    def _():
-        pl.semaphore_signal(ready_right, inc=1, device_id=left, device_id_type=MESH)
-
-    @pl.when(tan == ntan - 1)
-    def _():
-        pl.semaphore_signal(ready_left, inc=1, device_id=right, device_id_type=MESH)
-
-    far.wait_recv()
-
-    @pl.when(place < half - 1)
-    def _():
-        far_last.start()
 
     @pl.when(rad > 0)
     def _():
@@ -200,36 +217,29 @@
         for c in range(3):
             grid[c, 0] = grid[c, 1]
 
-    @pl.when(rad < nrad - 1)
-    def _():
-        to_below[0].wait_recv()
-
-    @pl.when(last)
-    def _():
-        for c in range(3):
-            grid[c, ROWS + 1] = grid[c, ROWS]
-
     step_in = length([grid[c, 1] for c in range(3)], [grid[c, 0] for c in range(3)])
-    step_out = length([grid[c, ROWS + 1] for c in range(3)], [grid[c, ROWS] for c in range(3)])
-
-    @pl.when(place > 0)
-    def _():
-        far_last.wait_recv()
-
-    @pl.when(place == 0)
+
+    pl.when(rad != half)(far_last.wait_recv)
+
+    @pl.when(rad == half)
     def _():
         for c in range(3):
             far_prior[c] = far_in[c]
 
     far_step = length([far_in[c] for c in range(3)], [far_prior[c] for c in range(3)])
     sums[place, 0] = step_in + top[3]
-    sums[place, 1] = far_in[6] + far_step + jnp.where(rad == half - 1, step_out, 0.0)
+    sums[place, 1] = far_in[6] + far_step
     sum_sends = [
         send(sums.at[place], sums.at[place], (sum_s, sum_r), k, device)
         for k, device in enumerate(peers)
     ]
     for copy in sum_sends:
         copy.start()
+
+    @pl.when(jnp.logical_not(turned))
+    def _():
+        for copy in bulk[AHEAD:]:
+            copy.start()
 
     @pl.when(rad == half)
     def _():
@@ -304,6 +314,16 @@
             def _():
                 walls[k + 1].wait_recv()
 
+    @pl.when(rad < nrad - 1)
+    def _():
+        to_below[0].wait_recv()
+
+    @pl.when(last)
+    def _():
+        for c in range(3):
+            grid[c, ROWS + 1] = grid[c, ROWS]
+
+    step_out = length([grid[c, ROWS + 1] for c in range(3)], [grid[c, ROWS] for c in range(3)])
     wall_y, wall_z = wall[0], wall[1]
     own_wall = [
         zero,
@@ -340,8 +360,7 @@
 
     def slab(src, dst, sems, k):
         size = ROWS // PARTS
-        extra = src.shape[0] - ROWS if k == PARTS - 1 else 0
-        part = pl.ds(k * size, size + extra)
+        part = pl.ds(k * size, size + (2 if k == PARTS - 1 else 0))
         return send(src.at[part], dst.at[part], sems, k, partner)
 
     frac_sends = [slab(frac_out, frac_in, (frac_s, frac_r), k) for k in range(PARTS)]
@@ -402,41 +421,32 @@
             z[2] * r[0] - z[0] * r[2],
             z[0] * r[1] - z[1] * r[0],
         ]
-        vol_out[j] = t[0] * face[0] + t[1] * face[1] + t[2] * face[2]
+        volume = t[0] * face[0] + t[1] * face[1] + t[2] * face[2]
+        if j < RAW:
+            vol_out[j] = volume
+        else:
+            for c in range(5):
+                product_out[c, j - RAW] = volume * flow[c, j + 2]
         mine, shift = row_of == j, (4 * j + 2) % 128
         return tuple(
             jnp.where(mine, pltpu.roll(face[c], shift, 1), packed[c]) for c in range(3)
         )
 
     face = each_row(slopes, (zero,) * 3)
-    vol_sends = [slab(vol_out, vol_in, (vol_s, vol_r), k) for k in range(PARTS)]
-    for copy in vol_sends:
-        copy.start()
-
-    @pl.when(rad > 0)
-    def _():
-        to_above[1].wait_recv()
-
-    @pl.when(first)
-    def _():
-        flow[:, 0:2] = jnp.zeros((5, 2, *TILE), jnp.float32)
-
-    @pl.when(rad < nrad - 1)
-    def _():
-        to_below[1].wait_recv()
-
-    @pl.when(last)
-    def _():
-        flow[:, ROWS + 2 : ROWS + 4] = jnp.zeros((5, 2, *TILE), jnp.float32)
-
-    def over_rad(j, carry):
-        odd, even = jst(*([flow[c, j + k] for c in range(5)] for k in range(5)))
-        for c in range(5):
-            odd_r[c, j] = odd[c]
-            even_r[c, j] = even[c]
-        return carry
-
-    lax.fori_loop(0, ROWS, over_rad, 0, unroll=2)
+    vol_sends = [send(vol_out, vol_in, (vol_s, vol_r), 0, partner)] + [
+        send(
+            product_out.at[:, pl.ds(j - RAW, 4)],
+            state_in.at[:, pl.ds(j, 4)],
+            (vol_s, vol_r), 1 + (j - RAW) // 4, partner,
+        )
+        for j in range(RAW, ROWS, 4)
+    ]
+    vol_sends[0].start()
+
+    @pl.when(turned)
+    def _():
+        for copy in vol_sends[1:]:
+            copy.start()
 
     for copy in edge_sends:
         copy.wait_recv()
@@ -446,9 +456,16 @@
         ahead = pltpu.roll(jnp.where(slot == 2, beside[5 + c], edges[c]), 127, 1)
         behind = pltpu.roll(jnp.where(slot == 1, beside[5 + c], edges[c]), 1, 1)
         rim.append((ahead - behind) * 0.5)
-    rim_out[...] = rim[0] * face[0] + rim[1] * face[1] + rim[2] * face[2]
+    rim_vol = rim[0] * face[0] + rim[1] * face[1] + rim[2] * face[2]
+    for c in range(5):
+        rim_out[c] = rim_vol * tight[c]
     rim_send = send(rim_out, rim_in, one, 3, partner)
     rim_send.start()
+
+    @pl.when(jnp.logical_not(turned))
+    def _():
+        for copy in vol_sends[1:]:
+            copy.start()
     m1, p1, m2, p2 = [], [], [], []
     for c in range(5):
         m2.append(jnp.where(slot < 2, wide[c], pltpu.roll(beside[c], 2, 1)))
@@ -458,6 +475,31 @@
         near = pltpu.roll(jnp.where(slot == 2, beside[c], tight[c]), 127, 1)
         p1.append(jnp.where(slot == 3, pltpu.roll(wide[c], 1, 1), near))
     rim_odd, rim_even = jst(m2, m1, tight, p1, p2)
+
+    @pl.when(rad > 0)
+    def _():
+        to_above[1].wait_recv()
+
+    @pl.when(first)
+    def _():
+        flow[:, 0:2] = jnp.zeros((5, 2, *TILE), jnp.float32)
+
+    @pl.when(rad < nrad - 1)
+    def _():
+        to_below[1].wait_recv()
+
+    @pl.when(last)
+    def _():
+        flow[:, ROWS + 2 : ROWS + 4] = jnp.zeros((5, 2, *TILE), jnp.float32)
+
+    def over_rad(j, carry):
+        odd, even = jst(*([flow[c, j + k] for c in range(5)] for k in range(5)))
+        for c in range(5):
+            odd_r[c, j] = odd[c]
+            even_r[c, j] = even[c]
+        return carry
+
+    lax.fori_loop(0, ROWS, over_rad, 0, unroll=2)
 
     loads[2].wait()
     for copy in frac_sends:
@@ -486,26 +528,34 @@
 
     each_row(fluxes, 0)
 
+    within = jnp.where(outer_one, 0.0, coef)
+    for copy in bulk + vol_sends[:1]:
+        copy.wait_recv()
+    for j in range(RAW):
+        weight = within * vol_in[j]
+        for c in range(5):
+            res_out[c, j] = res_out[c, j] + weight * state_in[c, j]
     rim_send.wait_recv()
-    rim_vol = rim_in[...]
-    for k in range(PARTS):
-        for copy in bulk[k * CHUNKS // PARTS : (k + 1) * CHUNKS // PARTS] + [vol_sends[k]]:
-            copy.wait_recv()
-        for j in range(k * ROWS // PARTS, (k + 1) * ROWS // PARTS):
-            shift = (126 - 4 * j) % 128
-            weight = coef * jnp.where(outer_one, pltpu.roll(rim_vol, shift, 1), vol_in[j])
-            for c in range(5):
-                res_out[c, j] = res_out[c, j] + weight * state_in[c, j]
+    for c in range(5):
+        rim_in[c] = coef * rim_in[c]
+    for j in range(ROWS):
+        for c in range(5):
+            edge = pltpu.roll(rim_in[c], (126 - 4 * j) % 128, 1)
+            res_out[c, j] = res_out[c, j] + jnp.where(outer_one, edge, 0.0)
+    for j in range(RAW, ROWS):
+        if j % 4 == 0:
+            vol_sends[1 + (j - RAW) // 4].wait_recv()
+        for c in range(5):
+            res_out[c, j] = res_out[c, j] + within * state_in[c, j]
 
     @pl.when(rad < nrad - 1)
     def _():
         for copy in to_above:
             copy.wait_send()
 
-    @pl.when(rad > 0)
-    def _():
-        for copy in to_below:
-            copy.wait_send()
+    pl.when((rad > 0) & (rad != half))(to_below[0].wait_send)
+    pl.when(first)(far_first.wait_send)
+    pl.when(rad > 0)(to_below[1].wait_send)
 
     @pl.when(first)
     def _():
@@ -517,9 +567,8 @@
         for copy in passed:
             copy.wait_send()
 
-    @pl.when(place < half - 1)
-    def _():
-        far_last.wait_send()
+    pl.when(place < half - 1)(far_last.wait_send)
+    pl.when(rad == half - 1)(near_last.wait_send)
 
     for copy in sum_sends + [far, rim_send] + edge_sends + frac_sends + vol_sends + bulk:
         copy.wait_send()
@@ -547,14 +596,14 @@
     dma = pltpu.SemaphoreType.DMA
     scratch = [
         tiles(3, ROWS + 2), tiles(5, ROWS + 4), tiles(5, ROWS), tiles(3, ROWS + 2), tiles(ROWS),
-        tiles(ROWS + 2), tiles(ROWS + 2), tiles(3, ROWS), tiles(3, ROWS), tiles(ROWS), tiles(ROWS),
+        tiles(ROWS + 2), tiles(ROWS + 2), tiles(3, ROWS), tiles(3, ROWS), tiles(RAW), tiles(RAW), tiles(5, ROWS - RAW),
         tiles(5, ROWS), tiles(5, ROWS), tiles(5, ROWS), tiles(5, ROWS), tiles(5, ROWS),
-        tiles(2), tiles(half, 2), tiles(7), tiles(7), tiles(3), tiles(8), tiles(8), tiles(8), tiles(), tiles(),
+        tiles(2), tiles(half, 2), tiles(7), tiles(7), tiles(3), tiles(8), tiles(8), tiles(8), tiles(5), tiles(5),
         pltpu.SMEM((2,), jnp.int32), pltpu.SMEM((2,), f32), pltpu.SMEM((3,), f32), pltpu.SMEM((3,), f32),
-        dma((7,)), dma((CHUNKS,)), dma((CHUNKS,)), dma((4,)), dma((4,)),
+        dma((7,)), dma((len(CUTS) - 1,)), dma((len(CUTS) - 1,)), dma((4,)), dma((4,)),
         dma((half,)), dma((half,)), dma((half - 1,)), dma((half - 1,)), dma((5,)), dma((5,)),
-        dma((PARTS,)), dma((PARTS,)), dma((PARTS,)), dma((PARTS,)),
-        pltpu.SemaphoreType.REGULAR, pltpu.SemaphoreType.REGULAR,
+        dma((PARTS,)), dma((PARTS,)), dma((1 + (ROWS - RAW) // 4,)), dma((1 + (ROWS - RAW) // 4,)),
+        *[pltpu.SemaphoreType.REGULAR] * 4,
     ]
     disp, res = pl.pallas_call(
         functools.partial(step_kernel, nrad, ntan),

time: 32.2 us -> 31.5 us (0.978)
  the two profiles are of different devices: /device:TPU:29 before, /device:TPU:1 now
where the time goes in v4:
time: 31.5 us; the launch traced here: 31.4 us
  Pallas kernels  30.7 us (97%)
  between operations  0.64 us (2%)
    pallas_call x1, Pallas kernels, body(): pl.pallas_call(functools.partial(step_kernel, nrad, ntan), out_shape=[jax...  29.8 us
    pallas_call x1, Pallas kernels, body(): pl.pallas_call(store_kernel, out_shape=[jax.ShapeDtypeStruct((1, 3, ROWS,...  0.99 us

profile of v4, /device:TPU:1, one launch (start us, length us, event | category | flops | bytes accessed | tf_op | source)
XLA Modules:
  0.0 31.4 jit_solution(16849568980712219109)
XLA Ops:
  0.6 29.8 %deform_and_residual.1 = (f32[3,32,8,128]{3,2,1,0:T(8,128)S(1)}, f32[5,32,8,128]{3,2,1,0:T(8,128)S(1)}) custom-call(f32[1,3,32,8,128]{4,3,2,1,0:T(8,128)} %coords.1, f32[1,5,32,8,128]{4,3,2,1,0:T(8,128)} %state.1, f32[1,5,32,8,128]{4,3,2,1,0:T(8,128)} %rest.1, s32[2]{0:T(128)} %ids.1, f32[2]{0:T(128)} %motion.1, f32[3]{0:T(128)} %heave.1, f32[3]{0:T(128)} %stream.1), custom_call_target="tpu_custom_call" | custom-call | tf_op jit(solution)/shard_map/deform_and_residual/pallas_call | solution.py:608
  30.4 1.0 %store_results.1 = (f32[1,3,32,8,128]{4,3,2,1,0:T(8,128)}, f32[1,5,32,8,128]{4,3,2,1,0:T(8,128)}) custom-call(f32[3,32,8,128]{3,2,1,0:T(8,128)S(1)} %get-tuple-element.4.disp, f32[5,32,8,128]{3,2,1,0:T(8,128)S(1)} %get-tuple-element.5.res), custom_call_target="tpu_custom_call" | custom-call | tf_op jit(solution)/shard_map/store_results/pallas_call | solution.py:622

commit v5 on v4

--- a/solution.py
+++ b/solution.py
@@ -199,6 +199,28 @@
         for copy in to_below:
             copy.start()
 
+    for load in loads[3:]:
+        load.wait()
+    own_id = jnp.where(inst == 0, ids_s[0], ids_s[1])
+    other_id = jnp.where(inst == 0, ids_s[1], ids_s[0])
+    offset_id = own_id - other_id
+    turn = 2.0 * jnp.pi / NINST
+    own_phase = turn * own_id.astype(jnp.float32) + motion_s[1]
+    other_phase = turn * other_id.astype(jnp.float32) + motion_s[1]
+    angle = (jnp.pi / NINST) * offset_id.astype(jnp.float32)
+    angles = jnp.where(span == 0, own_phase, jnp.where(span == 1, other_phase, angle))
+    sines, cosines = jnp.sin(angles), jnp.cos(angles)
+
+    def pick(values, k):
+        return jnp.broadcast_to(values[k : k + 1], TILE)
+
+    theta = motion_s[0] * pick(sines, 0)
+    sin_theta, cos_theta = jnp.sin(theta), jnp.cos(theta)
+    own_far = [heave_s[c] * pick(cosines, 0) for c in range(3)]
+    other_far = [heave_s[c] * pick(cosines, 1) for c in range(3)]
+    parity = 1.0 - 2.0 * lax.rem(offset_id + NINST, 2).astype(jnp.float32)
+    coef = 0.5 * parity * pick(cosines, 2) / pick(sines, 2)
+
     far.wait_recv()
     pl.when(place < half - 1)(far_last.start)
     pl.when(first)(far_first.start)
@@ -270,28 +292,6 @@
     tight, wide = packed[:5], packed[5:]
     for c in range(5):
         edge_out[c] = tight[c]
-
-    for load in loads[3:]:
-        load.wait()
-    own_id = jnp.where(inst == 0, ids_s[0], ids_s[1])
-    other_id = jnp.where(inst == 0, ids_s[1], ids_s[0])
-    offset_id = own_id - other_id
-    turn = 2.0 * jnp.pi / NINST
-    own_phase = turn * own_id.astype(jnp.float32) + motion_s[1]
-    other_phase = turn * other_id.astype(jnp.float32) + motion_s[1]
-    angle = (jnp.pi / NINST) * offset_id.astype(jnp.float32)
-    angles = jnp.where(span == 0, own_phase, jnp.where(span == 1, other_phase, angle))
-    sines, cosines = jnp.sin(angles), jnp.cos(angles)
-
-    def pick(values, k):
-        return jnp.broadcast_to(values[k : k + 1], TILE)
-
-    theta = motion_s[0] * pick(sines, 0)
-    sin_theta, cos_theta = jnp.sin(theta), jnp.cos(theta)
-    own_far = [heave_s[c] * pick(cosines, 0) for c in range(3)]
-    other_far = [heave_s[c] * pick(cosines, 1) for c in range(3)]
-    parity = 1.0 - 2.0 * lax.rem(offset_id + NINST, 2).astype(jnp.float32)
-    coef = 0.5 * parity * pick(cosines, 2) / pick(sines, 2)
 
     for copy in sum_sends:
         copy.wait_recv()

time: 31.5 us -> 31.5 us (level)
  no operation moved by 1% of the time
where the time goes in v5:
time: 31.5 us; the launch traced here: 31.4 us
  Pallas kernels  30.7 us (97%)
  between operations  0.64 us (2%)
    pallas_call x1, Pallas kernels, body(): pl.pallas_call(functools.partial(step_kernel, nrad, ntan), out_shape=[jax...  29.8 us
    pallas_call x1, Pallas kernels, body(): pl.pallas_call(store_kernel, out_shape=[jax.ShapeDtypeStruct((1, 3, ROWS,...  0.99 us

profile of v5, /device:TPU:1, one launch (start us, length us, event | category | flops | bytes accessed | tf_op | source)
XLA Modules:
  0.0 31.4 jit_solution(11441816260621972804)
XLA Ops:
  0.6 29.8 %deform_and_residual.1 = (f32[3,32,8,128]{3,2,1,0:T(8,128)S(1)}, f32[5,32,8,128]{3,2,1,0:T(8,128)S(1)}) custom-call(f32[1,3,32,8,128]{4,3,2,1,0:T(8,128)} %coords.1, f32[1,5,32,8,128]{4,3,2,1,0:T(8,128)} %state.1, f32[1,5,32,8,128]{4,3,2,1,0:T(8,128)} %rest.1, s32[2]{0:T(128)} %ids.1, f32[2]{0:T(128)} %motion.1, f32[3]{0:T(128)} %heave.1, f32[3]{0:T(128)} %stream.1), custom_call_target="tpu_custom_call" | custom-call | tf_op jit(solution)/shard_map/deform_and_residual/pallas_call | solution.py:608
  30.4 1.0 %store_results.1 = (f32[1,3,32,8,128]{4,3,2,1,0:T(8,128)}, f32[1,5,32,8,128]{4,3,2,1,0:T(8,128)}) custom-call(f32[3,32,8,128]{3,2,1,0:T(8,128)S(1)} %get-tuple-element.4.disp, f32[5,32,8,128]{3,2,1,0:T(8,128)S(1)} %get-tuple-element.5.res), custom_call_target="tpu_custom_call" | custom-call | tf_op jit(solution)/shard_map/store_results/pallas_call | solution.py:622
